TPU v7x, 32 devices: a whole 2x2x4 slice. The times are simulated.
32 devices in a mesh: seq: 8 (over z, x), wt: 4 (over y, core).
Axes of the slice: x: 2, y: 2, z: 4, core: 2. Of those that a mesh axis runs over, the one named last changes fastest.
Arguments:
- hidden: bfloat16 [4, 1536, 1536], P('wt', 'seq'), may hold values from -6 to 6
- cotangent: bfloat16 [4, 1536, 1536], P('wt', 'seq'), may hold values from -6 to 6
- segments: int32 [4, 1536], P('wt'), may hold values from 767 to 1535, as said below
- valid: int32 [4, 1536], P('wt', 'seq'), may hold values from 0 to 1
- in_w: float32 [1536, 6448], P(('seq', 'wt')), may hold values from -0.15625 to 0.15625
- in_m: float32 [1536, 6448], P(('seq', 'wt')), may hold values from -128 to 128
- in_v: float32 [1536, 6448], P(('seq', 'wt')), may hold values from 552.96 to 2211.84
- out_w: float32 [3072, 1536], P(('seq', 'wt')), may hold values from -0.109375 to 0.109375
- out_m: float32 [3072, 1536], P(('seq', 'wt')), may hold values from -384 to 384
- out_v: float32 [3072, 1536], P(('seq', 'wt')), may hold values from 3932.16 to 15728.64
- small_w: float32 [21392], replicated, may hold values from -8 to 1.5, as said below
- small_m: float32 [21392], replicated, may hold values from -313.5347 to 313.5347
- small_v: float32 [21392], replicated, may hold values from 245.76 to 24576
Outputs:
- output: bfloat16 [4, 1536, 1536], P('wt', 'seq')
- grad_hidden: float32 [4, 1536, 1536], P('wt', 'seq')
- in_m_new: float32 [1536, 6448], P(('seq', 'wt'))
- in_v_new: float32 [1536, 6448], P(('seq', 'wt'))
- in_w_new: float32 [1536, 6448], P(('seq', 'wt'))
- out_m_new: float32 [3072, 1536], P(('seq', 'wt'))
- out_v_new: float32 [3072, 1536], P(('seq', 'wt'))
- out_w_new: float32 [3072, 1536], P(('seq', 'wt'))
- small_m_new: float32 [21392], replicated
- small_v_new: float32 [21392], replicated
- small_w_new: float32 [21392], replicated
- rms: float32 [2], replicated
Inputs may be any that keep to these rules, and one draw needn't show every extreme that they name: `segments`: each token's number is the position, within its stream, of the last token of its document, so numbers never fall along a stream; a new document begins at every multiple of 4096; a document holds at most 2000 tokens; the first document of every stream holds between min(2000, 1536) // 2 and min(2000, 1336) tokens. `small_w`: in order: gains within 0.5 to 1.5, convolution weights and biases within -0.5 to 0.5, dt_bias within -8 to -3, a_log within 0 to 1.5, skip within 0.2 to 1.
All inputs are finite; a program needn't handle non-finite values.
Results may differ from a plain program's by a relative error of at most 0.0081.
The roundings to bfloat16 on the way count: a program that leaves them out, or rounds other values in their place, can miss the bound.
Values may be sent and summed in bfloat16 or wider, within the bound.
A program may use at most 256 MiB of HBM per device.

v0:
```python
import functools

import jax
import jax.numpy as jnp
from jax import lax
from jax.experimental import pallas as pl
from jax.experimental.pallas import tpu as pltpu
from jax.sharding import Mesh
from jax.sharding import PartitionSpec as P

D = 1536
D_INNER = 3072
HEADS = 48
HEADDIM = 64
STATE = 128
CONV = 4
SPAN = 256
STEP = 4
CONVCH = 3328
TP = 4
RIM = CONV - 1
LANES = 128
HALF = D_INNER // TP
LOCAL_HEADS = HEADS // TP
PAIRS = LOCAL_HEADS // 2
SIDE = 2 * STATE
COL_SIDE = HALF
COL_DT = HALF + SIDE
COL_GATE = COL_DT + LANES
COLS = COL_GATE + HALF

bf16 = jnp.bfloat16
f32 = jnp.float32
exact_prec = lax.Precision.HIGHEST
norm_eps = 1e-05
adam_eps = 1e-08


def dot(a, b, dims=((1,), (0,)), precision=None):
    return lax.dot_general(a, b, (dims, ((), ())), precision=precision, preferred_element_type=f32)


def unpack_small(small):
    first = D
    second = first + D_INNER
    third = second + CONV * CONVCH
    fourth = third + CONVCH
    fifth = fourth + HEADS
    sixth = fifth + HEADS
    return (
        small[:first],
        small[first:second],
        small[second:third].reshape(CONV, CONVCH),
        small[third:fourth],
        small[fourth:fifth],
        small[fifth:sixth],
        small[sixth:],
    )


def adamw(weight, moment, second, grad, rate, decay):
    moment_new = 0.5 * moment + 0.5 * grad
    second_new = 0.5 * second + 0.5 * grad * grad
    first_hat = moment_new / (1.0 - 0.5**STEP)
    second_hat = second_new / (1.0 - 0.5**STEP)
    weight_new = weight - rate * (first_hat / (jnp.sqrt(second_hat) + adam_eps) + decay * weight)
    return (moment_new, second_new, weight_new)


def pair_cols(cols, h):
    lane = lax.broadcasted_iota(jnp.int32, (cols.shape[0], LANES), 1)
    return jnp.where(lane < HEADDIM, cols[:, h : h + 1], cols[:, h + 1 : h + 2])


def span_rows(c):
    return pl.ds(pl.multiple_of(c * SPAN, SPAN), SPAN)


def span_decay(dt_ref, rate_ref, c, at=0):
    dt = dt_ref[span_rows(c), :]
    row = lax.broadcasted_iota(jnp.int32, (SPAN, SPAN), 0)
    col = lax.broadcasted_iota(jnp.int32, (SPAN, SPAN), 1)
    lower = (row >= col).astype(f32)
    return dt, dot(lower, dt * rate_ref[at : at + 1, :], precision=exact_prec)


def state_kernel(spans, x_ref, b_ref, dt_ref, rate_ref, keep_ref, carry_ref, s_ref, dec_ref):
    s_ref[...] = jnp.zeros_like(s_ref)
    dec_ref[...] = jnp.ones_like(dec_ref)

    def body(c, _):
        rows = span_rows(c)
        dt, cum = span_decay(dt_ref, rate_ref, c)
        last = cum[SPAN - 1 : SPAN, :]
        end_weight = jnp.exp(last - cum) * dt * keep_ref[rows, :]
        decay = jnp.exp(last) * carry_ref[pl.ds(c, 1), :]
        dec_ref[...] = dec_ref[...] * decay
        b = b_ref[rows, :]
        for p in range(PAIRS):
            lanes = slice(p * LANES, (p + 1) * LANES)
            xw = (x_ref[rows, lanes].astype(f32) * pair_cols(end_weight, 2 * p)).astype(bf16)
            fresh = dot(b, xw, ((0,), (0,)))
            s_ref[:, lanes] = s_ref[:, lanes] * pair_cols(decay, 2 * p) + fresh
        return 0

    lax.fori_loop(0, spans, body, 0)


def scan_kernel(
    spans, x_ref, b_ref, c_ref, dt_ref, rate_ref, segc_ref, segr_ref, keep_ref, inflow_ref, carry_ref, s_in_ref,
    y_ref, st_ref, s_ref,
):
    s_ref[...] = s_in_ref[...]

    def body(c, _):
        rows = span_rows(c)
        dt, cum = span_decay(dt_ref, rate_ref, c)
        last = cum[SPAN - 1 : SPAN, :]
        end_weight = jnp.exp(last - cum) * dt * keep_ref[rows, :]
        decay = jnp.exp(last) * carry_ref[pl.ds(c, 1), :]
        gain = jnp.exp(cum) * inflow_ref[rows, :]
        back_log = jnp.transpose(cum - jnp.log(dt))
        b = b_ref[rows, :]
        cc = c_ref[rows, :]
        scores = dot(cc, b, ((1,), (1,)))
        row = lax.broadcasted_iota(jnp.int32, (SPAN, SPAN), 0)
        col = lax.broadcasted_iota(jnp.int32, (SPAN, SPAN), 1)
        mask = (row >= col) & (segc_ref[rows, :] == segr_ref[pl.ds(c, 1), :])
        lane = lax.broadcasted_iota(jnp.int32, (SPAN, LANES), 1)
        st_ref[c] = s_ref[...]
        for p in range(PAIRS):
            lanes = slice(p * LANES, (p + 1) * LANES)
            x = x_ref[rows, lanes]
            parts = []
            for h in (2 * p, 2 * p + 1):
                gap = cum[:, h : h + 1] - back_log[h : h + 1, :]
                weights = scores * jnp.exp(jnp.where(mask, gap, -1e30))
                parts.append(dot(weights.astype(bf16), x))
            y = jnp.where(lane < HEADDIM, parts[0], parts[1])
            state = s_ref[:, lanes]
            y = y + dot(cc, state.astype(bf16)) * pair_cols(gain, 2 * p)
            y_ref[rows, lanes] = y
            xw = (x.astype(f32) * pair_cols(end_weight, 2 * p)).astype(bf16)
            s_ref[:, lanes] = state * pair_cols(decay, 2 * p) + dot(b, xw, ((0,), (0,)))
        return 0

    lax.fori_loop(0, spans, body, 0)


def state_back_kernel(spans, dy_ref, c_ref, dt_ref, rate_ref, inflow_ref, carry_ref, s_ref):
    s_ref[...] = jnp.zeros_like(s_ref)

    def body(step, _):
        c = spans - 1 - step
        rows = span_rows(c)
        dt, cum = span_decay(dt_ref, rate_ref, c)
        decay = jnp.exp(cum[SPAN - 1 : SPAN, :]) * carry_ref[pl.ds(c, 1), :]
        gain = jnp.exp(cum) * inflow_ref[rows, :]
        cc = c_ref[rows, :]
        for p in range(PAIRS):
            lanes = slice(p * LANES, (p + 1) * LANES)
            dyg = (dy_ref[rows, lanes].astype(f32) * pair_cols(gain, 2 * p)).astype(bf16)
            s_ref[:, lanes] = s_ref[:, lanes] * pair_cols(decay, 2 * p) + dot(cc, dyg, ((0,), (0,)))
        return 0

    lax.fori_loop(0, spans, body, 0)


def head_sums(values):
    width = values.shape[1]
    chan = lax.broadcasted_iota(jnp.int32, (width, LANES), 0)
    head = lax.broadcasted_iota(jnp.int32, (width, LANES), 1)
    pick = (chan // HEADDIM == head).astype(bf16)
    high = values.astype(bf16)
    low = (values - high.astype(f32)).astype(bf16)
    return dot(high, pick) + dot(low, pick)


def scan_back_kernel(
    spans, x_ref, b_ref, c_ref, dt_ref, ratio_ref, sig_ref, rate_ref, segc_ref, segr_ref, keep_ref, inflow_ref, carry_ref, skip_ref,
    y_ref, st_ref, dy_ref, ds_out_ref,
    dx_ref, db_ref, dc_ref, ddt_ref, drate_ref, dskip_ref,
    ds_ref, prod_ref,
):
    ds_ref[...] = ds_out_ref[...]
    drate_ref[...] = jnp.zeros_like(drate_ref)
    dskip_ref[...] = jnp.zeros_like(dskip_ref)

    def body(step, _):
        c = spans - 1 - step
        rows = span_rows(c)
        dt, cum = span_decay(dt_ref, rate_ref, c)
        last = cum[SPAN - 1 : SPAN, :]
        end_weight = jnp.exp(last - cum) * dt * keep_ref[rows, :]
        decay = jnp.exp(last) * carry_ref[pl.ds(c, 1), :]
        gain = jnp.exp(cum) * inflow_ref[rows, :]
        fore_log = jnp.transpose(cum)
        back_log = cum - jnp.log(dt)
        b = b_ref[rows, :]
        cc = c_ref[rows, :]
        scores = dot(b, cc, ((1,), (1,)))
        row = lax.broadcasted_iota(jnp.int32, (SPAN, SPAN), 0)
        col = lax.broadcasted_iota(jnp.int32, (SPAN, SPAN), 1)
        mask = (col >= row) & (segc_ref[rows, :] == segr_ref[pl.ds(c, 1), :])
        lane = lax.broadcasted_iota(jnp.int32, (SPAN, LANES), 1)
        d_scores = jnp.zeros((SPAN, SPAN), f32)
        db = jnp.zeros((SPAN, STATE), f32)
        dc = jnp.zeros((SPAN, STATE), f32)
        state_row = []
        dx_state_row = []
        for p in range(PAIRS):
            lanes = slice(p * LANES, (p + 1) * LANES)
            x = x_ref[rows, lanes]
            dy = dy_ref[rows, lanes]
            xf = x.astype(f32)
            dyf = dy.astype(f32)
            parts = []
            for k in range(2):
                h = 2 * p + k
                gap = fore_log[h : h + 1, :] - back_log[:, h : h + 1]
                decay_mat = jnp.exp(jnp.where(mask, gap, -1e30))
                weights = (scores * decay_mat).astype(bf16)
                parts.append(dot(weights, dy))
                own = (lane < HEADDIM) if k == 0 else (lane >= HEADDIM)
                d_weights = dot(jnp.where(own, xf, 0.0).astype(bf16), dy, ((1,), (1,)))
                d_scores = d_scores + d_weights * decay_mat
            dx = jnp.where(lane < HEADDIM, parts[0], parts[1])
            dyg = (dyf * pair_cols(gain, 2 * p)).astype(bf16)
            ew = pair_cols(end_weight, 2 * p)
            xw = (xf * ew).astype(bf16)
            state = st_ref[c, :, lanes]
            ds = ds_ref[:, lanes]
            state_b = state.astype(bf16)
            ds_b = ds.astype(bf16)
            dc = dc + dot(dyg, state_b, ((1,), (1,)))
            db = db + dot(xw, ds_b, ((1,), (1,)))
            dx_state = dot(b, ds_b) * ew
            dx = dx + dx_state
            dec = pair_cols(decay, 2 * p)
            state_row.append(jnp.sum(ds * state, axis=0, keepdims=True) * dec)
            dx_state_row.append(jnp.sum(dx_state * xf, axis=0, keepdims=True))
            ds_ref[:, lanes] = ds * dec + dot(cc, dyg, ((0,), (0,)))
            prod_ref[0:SPAN, lanes] = dyf * y_ref[rows, lanes]
            prod_ref[SPAN : 2 * SPAN, lanes] = xf * dx
            dskip_ref[0:1, lanes] += jnp.sum(dyf * xf, axis=0, keepdims=True)
            dx_ref[rows, lanes] = (dx + dyf * skip_ref[0:1, lanes]).astype(bf16)
        d_scores_b = d_scores.astype(bf16)
        db_ref[rows, :] = db + dot(d_scores_b, cc)
        dc_ref[rows, :] = dc + dot(d_scores_b, b, ((0,), (0,)))
        sums = head_sums(prod_ref[...])
        out_sum, in_sum = sums[:SPAN], sums[SPAN:]
        edge = jnp.concatenate(state_row, axis=1) + jnp.concatenate(dx_state_row, axis=1)
        edge_sum = head_sums(jnp.broadcast_to(edge, (8, HALF)))[0:1]
        at_last = lax.broadcasted_iota(jnp.int32, (SPAN, LANES), 0) == SPAN - 1
        d_cum = out_sum - in_sum + jnp.where(at_last, edge_sum, 0.0)
        upper = (col >= row).astype(f32)
        d_log = dot(upper, d_cum, precision=exact_prec)
        drate_ref[0:1, :] += jnp.sum(d_log * dt, axis=0, keepdims=True)
        ddt_ref[rows, :] = d_log * rate_ref[0:1, :] * sig_ref[rows, :] + in_sum * ratio_ref[rows, :]
        return 0

    lax.fori_loop(0, spans, body, 0)


GROUP = ("t1", "t0")
COPIES = ("part", "w1", "w0")
EVERYONE = ("part", "t1", "t0", "w1", "w0")


VMEM_LIMIT = 63 * 1024 * 1024


def in_vmem(kernel, out_shape, name, scratch=()):
    return pl.pallas_call(
        kernel,
        out_shape=out_shape,
        scratch_shapes=list(scratch),
        name=name,
        compiler_params=pltpu.CompilerParams(vmem_limit_bytes=VMEM_LIMIT),
    )


def shape(dims, dtype):
    return jax.ShapeDtypeStruct(dims, dtype)


def shift_part(array, by):
    size = lax.axis_size("part")
    pairs = [(i, i + by) for i in range(size) if 0 <= i + by < size]
    return lax.ppermute(array, "part", pairs)


def shards_general(
    hidden, cotangent, segments, valid, in_w, in_m, in_v, out_w, out_m, out_v, small_w, small_m, small_v,
):
    parts = lax.axis_size("part")
    wt = lax.axis_size("w1") * lax.axis_size("w0")
    part = lax.axis_index("part")
    tp = lax.axis_index("t1") * 2 + lax.axis_index("t0")
    own_rows = in_w.shape[0]
    out_rows = out_w.shape[0]
    resid = hidden[0].astype(f32)
    tok_rows = resid.shape[0]
    rows = tok_rows * TP
    spans = rows // SPAN
    seg_all = segments[0]
    pre_gain, norm_gain, conv_weight, conv_bias, dt_shift, a_logs, skips = unpack_small(small_w)

    def own_part(array, width):
        return lax.dynamic_slice_in_dim(array, tp * width, width, array.ndim - 1)

    in_copy = in_w.astype(bf16)
    slices = []
    for j in range(TP):
        slices.append(
            jnp.concatenate(
                [
                    in_copy[:, D_INNER + j * HALF : D_INNER + (j + 1) * HALF],
                    in_copy[:, 2 * D_INNER : 2 * D_INNER + SIDE],
                    in_copy[:, D_INNER + CONVCH + j * LOCAL_HEADS : D_INNER + CONVCH + (j + 1) * LOCAL_HEADS],
                    jnp.zeros((own_rows, LANES - LOCAL_HEADS), bf16),
                    in_copy[:, j * HALF : (j + 1) * HALF],
                ],
                axis=1,
            )
        )
    mine = lax.all_to_all(jnp.stack(slices), GROUP, 0, 0, tiled=False)
    w_in = lax.all_gather(mine, COPIES, axis=0, tiled=False)
    w_in = w_in.reshape(parts, wt, TP, own_rows, COLS).transpose(0, 2, 1, 3, 4).reshape(D, COLS)
    flat = [(i, (i % TP) * parts + i // TP) for i in range(parts * TP)]
    out_mine = lax.ppermute(out_w.astype(bf16), ("part", *GROUP), [(b, a) for a, b in flat])
    w_out = lax.all_gather(out_mine, COPIES, axis=0, tiled=True)

    hidden_all = lax.all_gather(hidden[0], GROUP, axis=0, tiled=True)
    back_mix = cotangent[0] * valid[0][:, None].astype(bf16)
    back_all = lax.all_gather(back_mix, GROUP, axis=0, tiled=True)

    hid = hidden_all.astype(f32)
    scale_all = lax.rsqrt(jnp.mean(hid * hid, axis=1, keepdims=True) + norm_eps)
    x_normed = (hid * scale_all * pre_gain).astype(bf16)
    projected = dot(x_normed, w_in)
    conv_in = projected[:, :COL_DT].astype(bf16)
    dt_raw = projected[:, COL_DT:COL_GATE].astype(bf16).astype(f32)
    gate_pre = projected[:, COL_GATE:]
    rim_in = shift_part(conv_in[rows - RIM :], 1)
    padded = jnp.concatenate([rim_in, conv_in], axis=0).astype(f32)
    seg_front = jnp.concatenate([jnp.full((RIM,), -1, jnp.int32), seg_all, jnp.full((RIM,), -1, jnp.int32)])
    seg_pad = lax.dynamic_slice_in_dim(seg_front, part * rows, rows + 2 * RIM)
    seg = seg_pad[RIM : RIM + rows]
    masks = [(seg_pad[k : k + rows] == seg).astype(f32)[:, None] for k in range(CONV)]
    taps = jnp.concatenate([own_part(conv_weight[:, :D_INNER], HALF), conv_weight[:, D_INNER:]], axis=1)
    bias = jnp.concatenate([own_part(conv_bias[:D_INNER], HALF), conv_bias[D_INNER:]])
    total = bias[None, :]
    for k in range(CONV):
        total = total + taps[k] * padded[k : k + rows] * masks[k]
    sig_total = jax.nn.sigmoid(total)
    activated = (total * sig_total).astype(bf16)
    x_scan = activated[:, :HALF]
    b_mat = activated[:, HALF : HALF + STATE]
    c_mat = activated[:, HALF + STATE :]

    def head_row(array):
        return jnp.pad(own_part(array, LOCAL_HEADS), (0, LANES - LOCAL_HEADS))

    shift_row = head_row(dt_shift)
    z = dt_raw + shift_row
    dt = jax.nn.softplus(z)
    sig_dt = jax.nn.sigmoid(z)
    ratio = jnp.where(dt > 1e-30, sig_dt / jnp.maximum(dt, 1e-30), 1.0)
    rate_row = -jnp.exp(head_row(a_logs))
    rate8 = jnp.broadcast_to(rate_row, (8, LANES))
    skip_chan = jnp.repeat(own_part(skips, LOCAL_HEADS), HEADDIM)
    skip8 = jnp.broadcast_to(skip_chan, (8, HALF))
    seg_spans = seg.reshape(spans, SPAN)
    seg_last = seg_spans[:, -1]
    seg_before = jnp.concatenate([seg_pad[RIM - 1 : RIM], seg_last[:-1]])
    keep = (seg_spans == seg_last[:, None]).astype(f32).reshape(rows, 1)
    inflow = (seg_spans == seg_before[:, None]).astype(f32).reshape(rows, 1)
    carry = jnp.broadcast_to((seg_last == seg_before).astype(f32)[:, None], (spans, LANES))
    seg_col = seg[:, None]

    state_shape = shape((STATE, HALF), f32)
    s_local, dec_total = in_vmem(
        functools.partial(state_kernel, spans), (state_shape, shape((8, LANES), f32)), "state"
    )(x_scan, b_mat, dt, rate8, keep, carry)
    dec_chan = jnp.repeat(dec_total[0, :LOCAL_HEADS], HEADDIM)
    s_in = jnp.zeros((STATE, HALF), f32)
    for _ in range(parts - 1):
        s_in = shift_part(dec_chan * s_in + s_local, 1)
    y_scan, states = in_vmem(
        functools.partial(scan_kernel, spans),
        (shape((rows, HALF), f32), shape((spans, STATE, HALF), f32)),
        "scan",
        [pltpu.VMEM((STATE, HALF), f32)],
    )(x_scan, b_mat, c_mat, dt, rate8, seg_col, seg_spans, keep, inflow, carry, s_in)
    y_b = (y_scan + skip_chan * x_scan.astype(f32)).astype(bf16).astype(f32)

    gain_own = own_part(norm_gain, HALF)
    sig_gate = jax.nn.sigmoid(gate_pre)
    silu_gate = gate_pre * sig_gate
    gated = y_b * silu_gate
    gate_sq = lax.psum(jnp.sum(gated * gated, axis=1), GROUP)
    scale_gate = lax.rsqrt(gate_sq / D_INNER + norm_eps)[:, None]
    normed = (gated * scale_gate * gain_own).astype(bf16)
    mixer = lax.psum_scatter(dot(normed, w_out), GROUP, scatter_dimension=0, tiled=True)
    output = (resid + mixer).astype(bf16)
    valid_rows = valid[0].astype(f32)
    res_sq = jnp.sum(valid_rows * jnp.sum(resid * resid, axis=1))
    mix_sq = jnp.sum(valid_rows * jnp.sum(mixer * mixer, axis=1))
    valid_count = jnp.sum(valid_rows)

    d_normed = dot(back_all, w_out, ((1,), (1,)))
    g_out = dot(normed, back_all, ((0,), (0,)))
    g_out = lax.psum_scatter(g_out, COPIES, scatter_dimension=0, tiled=True)
    g_out = lax.ppermute(g_out, ("part", *GROUP), flat)
    d_gain = d_normed * gain_own
    gate_dot = lax.psum(jnp.sum(gated * d_gain, axis=1), GROUP)
    d_gated = scale_gate * d_gain - gated * (scale_gate**3 * (gate_dot / D_INNER)[:, None])
    d_norm_gain = jnp.sum(gated * scale_gate * d_normed, axis=0)
    dy = (d_gated * silu_gate).astype(bf16)
    d_gate = d_gated * y_b * (sig_gate * (1.0 + gate_pre * (1.0 - sig_gate)))

    ds_local = in_vmem(functools.partial(state_back_kernel, spans), state_shape, "state_back")(
        dy, c_mat, dt, rate8, inflow, carry
    )
    ds_out = jnp.zeros((STATE, HALF), f32)
    for _ in range(parts - 1):
        ds_out = shift_part(dec_chan * ds_out + ds_local, -1)
    d_x, d_b, d_c, d_dt, d_rate, d_skip = in_vmem(
        functools.partial(scan_back_kernel, spans),
        (
            shape((rows, HALF), bf16),
            shape((rows, STATE), f32),
            shape((rows, STATE), f32),
            shape((rows, LANES), f32),
            shape((8, LANES), f32),
            shape((8, HALF), f32),
        ),
        "scan_back",
        [pltpu.VMEM((STATE, HALF), f32), pltpu.VMEM((2 * SPAN, HALF), f32)],
    )(x_scan, b_mat, c_mat, dt, ratio, sig_dt, rate8, seg_col, seg_spans, keep, inflow, carry, skip8, y_scan, states, dy, ds_out)

    d_total = jnp.concatenate([d_x.astype(f32), d_b, d_c], axis=1) * (sig_total * (1.0 + total * (1.0 - sig_total)))
    rim_back = shift_part(d_total[:RIM], -1)
    d_padded = jnp.concatenate([d_total, rim_back], axis=0)
    d_conv_in = 0.0
    for k in range(CONV):
        later = (seg_pad[2 * RIM - k : 2 * RIM - k + rows] == seg).astype(f32)[:, None]
        d_conv_in = d_conv_in + taps[k] * d_padded[RIM - k : RIM - k + rows] * later
    d_taps = jnp.stack([jnp.sum(d_total * padded[k : k + rows] * masks[k], axis=0) for k in range(CONV)])
    d_bias = jnp.sum(d_total, axis=0)
    d_proj = jnp.concatenate([d_conv_in, d_dt, d_gate], axis=1).astype(bf16)
    d_x_normed = dot(d_proj, w_in, ((1,), (1,)))
    d_x_normed = lax.psum_scatter(d_x_normed, GROUP, scatter_dimension=0, tiled=True)
    g_in = dot(x_normed, d_proj, ((0,), (0,)))
    g_in = g_in.reshape(parts, TP, wt, own_rows, COLS).transpose(0, 2, 1, 3, 4).reshape(parts * wt, TP, own_rows, COLS)
    g_in = lax.psum_scatter(g_in, COPIES, scatter_dimension=0, tiled=False)
    g_in = lax.all_to_all(g_in, GROUP, 0, 0, tiled=False)
    g_in = jnp.concatenate(
        [g_in[j, :, COL_GATE:] for j in range(TP)]
        + [g_in[j, :, :HALF] for j in range(TP)]
        + [jnp.sum(g_in[:, :, COL_SIDE:COL_DT], axis=0)]
        + [g_in[j, :, COL_DT : COL_DT + LOCAL_HEADS] for j in range(TP)],
        axis=1,
    )

    scale_own = lax.rsqrt(jnp.mean(resid * resid, axis=1, keepdims=True) + norm_eps)
    d_pre = d_x_normed * pre_gain
    dot_pre = jnp.mean(resid * d_pre, axis=1, keepdims=True)
    grad_hidden = back_mix.astype(f32) + scale_own * d_pre - resid * (scale_own**3 * dot_pre)
    d_pre_gain = jnp.sum(resid * scale_own * d_x_normed, axis=0)

    def placed(values, width):
        spread = (jnp.arange(TP) == tp).astype(f32)[:, None] * values[..., None, :]
        return spread.reshape(*values.shape[:-1], TP * width)

    d_weight = jnp.concatenate([placed(d_taps[:, :HALF], HALF), d_taps[:, HALF:]], axis=1)
    small_grad = jnp.concatenate(
        [
            d_pre_gain,
            placed(d_norm_gain, HALF),
            d_weight.reshape(-1),
            placed(d_bias[:HALF], HALF),
            d_bias[HALF:],
            placed(jnp.sum(d_dt, axis=0)[:LOCAL_HEADS], LOCAL_HEADS),
            placed((d_rate[0] * rate_row)[:LOCAL_HEADS], LOCAL_HEADS),
            placed(jnp.sum(d_skip[0].reshape(LOCAL_HEADS, HEADDIM), axis=1), LOCAL_HEADS),
            jnp.stack([res_sq, mix_sq, valid_count]),
        ]
    )
    small_total = lax.psum(small_grad, EVERYONE)
    res_total, mix_total, count_total = small_total[-3], small_total[-2], small_total[-1]
    in_m_new, in_v_new, in_w_new = adamw(in_w, in_m, in_v, g_in, 0.02, 0.1)
    out_m_new, out_v_new, out_w_new = adamw(out_w, out_m, out_v, g_out, 0.02, 0.1)
    small_m_new, small_v_new, small_w_new = adamw(small_w, small_m, small_v, small_total[:-3], 0.2, 0.0)
    rms = jnp.stack([jnp.sqrt(res_total / (count_total * D)), jnp.sqrt(mix_total / (count_total * D))])
    return (
        output[None], grad_hidden[None], in_m_new, in_v_new, in_w_new, out_m_new, out_v_new, out_w_new,
        small_m_new, small_v_new, small_w_new, rms,
    )


MESH = pl.DeviceIdType.MESH
T0, T1, DIAG, CORE, SIDEWAYS, PART = ("t0",), ("t1",), ("t1", "t0"), ("w0",), ("w1",), ("part",)
SIDE_CORE = ("w1", "w0")
HOPS = (None, T0, T1, DIAG)
HBM = pl.BlockSpec(memory_space=pl.ANY)
VMEM = pl.BlockSpec(memory_space=pltpu.VMEM)
MAIN = COL_GATE
CHANS = HALF + SIDE
FRONT = 16
TILE = 8
QUARTER = HALF // 2
NORM_ROW = D // LANES
TAP_ROW = NORM_ROW + D_INNER // LANES
TAP_ROWS = CONVCH // LANES
HEAD_ROW = TAP_ROW + (CONV + 1) * TAP_ROWS
SMALL_ROWS = HEAD_ROW + 2
BOX_ROWS = SMALL_ROWS + 8
OWN_NORM = NORM_ROW
OWN_TAP = OWN_NORM + HALF // LANES
OWN_SIDE = OWN_TAP + (CONV + 1) * (HALF // LANES)
OWN_HEAD = OWN_SIDE + (CONV + 1) * (SIDE // LANES)
OWN_SUMS = OWN_HEAD + 3
OWN_ROWS = 64


def place():
    return tuple(lax.axis_index(a) for a in EVERYONE)


def across(flips):
    return {a: 1 - lax.axis_index(a) for a in flips}


def group_blocks():
    _, t1, t0, _, _ = place()
    return [(t1, t0), (t1, 1 - t0), (1 - t1, t0), (1 - t1, 1 - t0)]


def greet(neighbours):
    barrier = pltpu.get_barrier_semaphore()
    for flips in neighbours:
        pl.semaphore_signal(barrier, inc=1, device_id=across(flips), device_id_type=MESH)


def greeted(neighbours):
    pl.semaphore_wait(pltpu.get_barrier_semaphore(), len(neighbours))


class Copies:
    def __init__(self, local_sem, send_sem, recv_sem):
        self.local_sem, self.send_sem, self.recv_sem = local_sem, send_sem, recv_sem
        self.sent, self.kept, self.in_flight, self.on_device = 0, 0, [], []

    def send(self, src, dst, flips):
        copy = pltpu.make_async_remote_copy(
            src_ref=src,
            dst_ref=dst,
            send_sem=self.send_sem.at[self.sent],
            recv_sem=self.recv_sem.at[self.sent],
            device_id=across(flips),
            device_id_type=MESH,
        )
        copy.start()
        self.sent += 1
        self.in_flight.append(copy)
        return copy

    def keep(self, src, dst):
        copy = pltpu.make_async_copy(src, dst, self.local_sem.at[self.kept])
        copy.start()
        self.kept += 1
        self.on_device.append(copy)
        return copy

    def settle(self, copy):
        copy.wait()
        self.on_device = [other for other in self.on_device if other is not copy]

    def left(self, copies):
        for copy in copies:
            copy.wait_send()
            self.in_flight = [other for other in self.in_flight if other is not copy]

    def drain(self):
        for copy in self.in_flight:
            copy.wait_send()
        for copy in self.on_device:
            copy.wait()
        self.in_flight, self.on_device = [], []


def sems(remote, local=1):
    return [
        pltpu.SemaphoreType.DMA((local,)),
        pltpu.SemaphoreType.DMA((remote,)),
        pltpu.SemaphoreType.DMA((remote,)),
    ]


class GroupGather:
    def __init__(self, copies, src, dst):
        self.copies, self.dst = copies, dst
        self.rows = src.shape[0]
        self.halves = (0, self.rows // 2)
        own = group_blocks()[0]
        self.own = copies.keep(src, self.at(own, 0, self.rows))
        size = self.rows // 2
        self.along_t1 = [copies.send(src.at[pl.ds(h, size)], self.at(own, h, size), T1) for h in self.halves]
        self.along_t0 = [copies.send(src.at[pl.ds(h, size)], self.at(own, h, size), T0) for h in self.halves]
        self.diagonal = []

    def at(self, block, first, size):
        return self.dst.at[pl.ds(pl.multiple_of((block[0] * 2 + block[1]) * self.rows + first, size), size)]

    def hand_on(self):
        beside = group_blocks()[2]
        for copy, h in zip(self.along_t1, self.halves):
            copy.wait_recv()
            here = self.at(beside, h, self.rows // 2)
            self.diagonal.append(self.copies.send(here, here, T0))

    def finish(self):
        for copy in self.along_t0 + self.diagonal:
            copy.wait_recv()


class WeightGather:
    def __init__(self, copies, dst, rows, group):
        self.copies, self.dst, self.rows, self.group = copies, dst, rows, group
        self.by_part, self.by_side, self.by_core = [], [], []

    def at(self, part, w1, w0, block):
        index = part
        if self.group:
            index = (index * 2 + block[0]) * 2 + block[1]
        index = (index * 2 + w1) * 2 + w0
        return self.dst.at[pl.ds(pl.multiple_of(index * self.rows, self.rows), self.rows)]

    def mine(self, block):
        p, _, _, w1, w0 = place()
        return self.at(p, w1, w0, block)

    def spread(self, src, block):
        dst = self.mine(block)
        self.by_part.append((self.copies.send(src, dst, PART), block))
        self.by_side.append((self.copies.send(src, dst, SIDEWAYS), block))
        self.by_core.append(self.copies.send(src, dst, CORE))

    def swap(self, src):
        own, *others = group_blocks()

        def slice_of(block):
            return src.at[block_rows(block, self.rows)]

        self.swaps = [(self.copies.send(slice_of(b), self.mine(own), flips), b) for b, flips in zip(others, HOPS[1:])]
        self.kept = self.copies.keep(slice_of(own), self.mine(own))
        self.spread(slice_of(own), own)

    def spread_swapped(self):
        for copy, block in self.swaps:
            copy.wait_recv()
            self.spread(self.mine(block), block)

    def pass_core(self, part, w1, block):
        here = self.at(part, w1, lax.axis_index("w0"), block)
        self.by_core.append(self.copies.send(here, here, CORE))

    def hand_on(self):
        p, _, _, w1, w0 = place()
        self.again = []
        for (copy, block), (side, _) in zip(self.by_part, self.by_side):
            side.wait_recv()
            self.pass_core(p, 1 - w1, block)
            copy.wait_recv()
            here = self.at(1 - p, w1, w0, block)
            self.again.append((self.copies.send(here, here, SIDEWAYS), block))
            self.pass_core(1 - p, w1, block)

    def hand_on_last(self):
        p, _, _, w1, _ = place()
        for copy, block in self.again:
            copy.wait_recv()
            self.pass_core(1 - p, 1 - w1, block)

    def finish(self):
        for copy in self.by_core:
            copy.wait_recv()


class GradientSum:
    def __init__(self, copies, srcs, rows, bufs, group):
        self.copies, self.srcs, self.rows, self.group = copies, srcs, rows, group
        self.core, self.sides, self.fars = bufs[:3]
        self.lasts = bufs[3] if group else None
        self.blocks = group_blocks() if group else [()]
        self.order = (1, 2, 3, 0) if group else (0,)
        p, _, _, w1, _ = place()
        self.parts, self.sides_of = (1 - p, p), (1 - w1, w1)
        self.core_copies, self.side_copies, self.far_copies, self.last_copies = {}, {}, {}, {}

    def at(self, block, side, w0):
        index = block[0] * 2 + block[1] if self.group else 0
        index = (index * 2 + side) * 2 + w0
        return pl.ds(pl.multiple_of(index * self.rows, self.rows), self.rows)

    def place(self, i, j):
        return self.at(self.blocks[i], self.sides_of[j], lax.axis_index("w0"))

    def pass_on(self, k, i, j, value, dst, flips):
        here = self.place(i, j)
        self.srcs[k][here, :] = value.astype(bf16)
        return self.copies.send(self.srcs[k].at[here], dst, flips)

    def added(self, k, i, j, *more):
        q, block, side = self.parts[k], self.blocks[i], self.sides_of[j]
        self.core_copies[k, i, j].wait_recv()
        value = self.srcs[k][self.place(i, j), :].astype(f32)
        value = value + self.core[(q, side, *block)].astype(f32)
        for other in more:
            value = value + other.astype(f32)
        return value

    def cores(self, k):
        w0 = lax.axis_index("w0")
        for j in range(2):
            for i in self.order:
                q, block, side = self.parts[k], self.blocks[i], self.sides_of[j]
                src = self.srcs[k].at[self.at(block, side, 1 - w0)]
                self.core_copies[k, i, j] = self.copies.send(src, self.core.at[(q, side, *block)], CORE)

    def left(self):
        for copies in (self.core_copies, self.side_copies, self.far_copies, self.last_copies):
            self.copies.left(copies.values())

    def to_sides(self, k):
        for i in self.order:
            self.side_copies[k, i] = self.pass_on(k, i, 0, self.added(k, i, 0), self.sides.at[k, i], SIDEWAYS)

    def to_part(self, which=None):
        for i in self.order if which is None else which:
            self.side_copies[0, i].wait_recv()
            value = self.added(0, i, 1, self.sides[0, i])
            self.far_copies[i] = self.pass_on(0, i, 1, value, self.fars.at[i], PART)

    def total(self, i):
        self.side_copies[1, i].wait_recv()
        self.far_copies[i].wait_recv()
        return self.added(1, i, 1, self.sides[1, i], self.fars[i])

    def to_group(self, store):
        for i in self.order:
            value = self.total(i)
            if i == 0:
                store(0, value)
            else:
                self.last_copies[i] = self.pass_on(1, i, 1, value, self.lasts.at[i - 1], HOPS[i])

    def finish(self, store):
        for i, copy in self.last_copies.items():
            copy.wait_recv()
            store(i, self.lasts[i - 1].astype(f32))


class GroupScatter:
    def __init__(self, copies, src, bufs):
        self.copies, self.src = copies, src
        self.here, self.pass_on, self.last = bufs
        self.rows = self.here.shape[0]

    def block(self, i):
        return block_rows(group_blocks()[i], self.rows)

    def left(self):
        self.copies.left([self.own_copy, self.pass_copy])

    def to_t0(self, i):
        copy = self.copies.send(self.src.at[self.block(i)], self.here if i == 1 else self.pass_on, T0)
        if i == 1:
            self.own_copy = copy
        else:
            self.pass_copy = copy

    def to_t1(self):
        self.pass_copy.wait_recv()
        here = self.block(2)
        self.src[here, :] = (self.src[here, :].astype(f32) + self.pass_on[...].astype(f32)).astype(bf16)
        self.last_copy = self.copies.send(self.src.at[here], self.last, T1)

    def finish(self):
        self.own_copy.wait_recv()
        self.last_copy.wait_recv()
        return self.here[...].astype(f32) + self.last[...].astype(f32)


def scatter_buffers(rows):
    return [pltpu.VMEM((rows, D), bf16)] * 3


def sum_buffers(rows, cols, group):
    buf = lambda *lead: pltpu.VMEM((*lead, rows, cols), bf16)
    if not group:
        return [buf(2, 2), buf(2, 1), buf(1)]
    return [buf(2, 2, 2, 2), buf(2, 4), buf(4), buf(3)]


def block_rows(block, size):
    return pl.ds(pl.multiple_of((block[0] * 2 + block[1]) * size, size), size)


def lane_of(h):
    return h if h < LOCAL_HEADS // 2 else h + HEADS // 2 - LOCAL_HEADS // 2


def own_pair(cols, h):
    lane = lax.broadcasted_iota(jnp.int32, (cols.shape[0], LANES), 1)
    first, second = lane_of(h), lane_of(h + 1)
    return jnp.where(lane < HEADDIM, cols[:, first : first + 1], cols[:, second : second + 1])


def own_sums(values):
    width = values.shape[1]
    head = lax.broadcasted_iota(jnp.int32, (width, LANES), 0) // HEADDIM
    lane = lax.broadcasted_iota(jnp.int32, (width, LANES), 1)
    pick = (jnp.where(head < LOCAL_HEADS // 2, head, head + lane_of(LOCAL_HEADS) - LOCAL_HEADS) == lane).astype(bf16)
    high = values.astype(bf16)
    low = (values - high.astype(f32)).astype(bf16)
    return dot(high, pick) + dot(low, pick)


def head_lanes(values, back=False):
    first = (lax.axis_index("t1") * 2 + lax.axis_index("t0")) * (LOCAL_HEADS // 2)
    return pltpu.roll(values, first if back else LANES - first, 1)


def own_row(first, k):
    tp = lax.axis_index("t1") * 2 + lax.axis_index("t0")
    third = QUARTER // LANES
    return pl.ds(first + (k // third) * (D_INNER // 2 // LANES) + tp * third + k % third, 1)


def own_chans(j):
    return [slice(first + j * QUARTER, first + (j + 1) * QUARTER) for first in (0, D_INNER // 2)]


EVERY_NEIGHBOUR = (T0, T1, DIAG, CORE, SIDEWAYS, SIDE_CORE, PART)


def main_kernel(
    spans, hid_ref, inw_hbm, outw_hbm, cot_hbm, inside_ref, valid_ref, small_ref, segc_ref, segr_ref,
    cotv_out, mixer_out, ggate_out, gmain_out, dx_out, gout_out, total_ref,
    h_ref, xn_ref, win_ref, convp_ref, x_ref, b_ref, c_ref, dtot_ref, dt_ref, z_ref, cum_ref, y_ref, st_ref,
    wgate_ref, wout_ref, back_ref, normed_ref, mix_ref, dy_ref, dgate_ref, dmain_ref, dgain_ref, taps_ref, heads_ref, chans_ref,
    marks_ref, carry_ref, s_ref, pass_ref, got_ref, rim_ref, gated_ref, gate_ref, dn_ref,
    stat_ref, stats_ref, dyg_ref, passb_ref, gotb_ref, rims_ref, rimr_ref, hsum_ref, dskip_ref, dtaps_ref,
    dpre_ref, box_ref, boxes_ref, gm_ref,
    *rest,
):
    go_bufs, gg_bufs, gm_bufs, mix_bufs, dx_bufs = rest[:3], rest[3:7], rest[7:11], rest[11:14], rest[14:17]
    local_sem, send_sem, recv_sem = rest[17:]
    greet(EVERY_NEIGHBOUR)
    p, _, _, _, _ = place()
    rows_all = spans * SPAN
    tokens = hid_ref.shape[0]
    own_rows, out_rows = inw_hbm.shape[0], outw_hbm.shape[0]
    lane = lax.broadcasted_iota(jnp.int32, (1, LANES), 1)
    wm_ref = dmain_ref.at[pl.ds(0, TP * own_rows)]
    wg_ref = dgate_ref.at[pl.ds(0, TP * own_rows)]
    wo_ref = mix_ref.at[pl.ds(0, out_rows)]
    cotv_ref = mix_ref.at[pl.ds(tokens, tokens)]
    dxi_ref, prod_ref = gated_ref, gate_ref

    def side_at(c, which):
        return (slice(spans * STATE, spans * STATE + SPAN), pl.ds(pl.multiple_of((which * spans + c) * STATE, STATE), STATE))


    copies = Copies(local_sem, send_sem, recv_sem)
    loads = [
        copies.keep(inw_hbm.at[:, pl.ds(k * HALF, HALF)], gate_ref.at[pl.ds(k * own_rows, own_rows)])
        for k in range(2 * D_INNER // HALF)
    ]
    loads += [
        copies.keep(outw_hbm.at[:, pl.ds(k * HALF, HALF)], dn_ref.at[pl.ds(k * out_rows, out_rows)]) for k in range(D // HALF)
    ]
    loads.append(copies.keep(cot_hbm, cotv_ref))

    side = inside_ref[...]
    dt_cols = jnp.concatenate([side[:, SIDE:], jnp.zeros((own_rows, LANES - HEADS), f32)], axis=1)
    for copy in loads:
        copies.settle(copy)
    cotv_ref[...] = (cotv_ref[...].astype(f32) * valid_ref[...]).astype(bf16)

    def master(first):
        return gate_ref[first // HALF * own_rows : (first // HALF + 1) * own_rows, first % HALF : first % HALF + QUARTER]

    for j in range(TP):
        at = slice(j * own_rows, (j + 1) * own_rows)
        for k, chans in enumerate(own_chans(j)):
            part = slice(k * QUARTER, (k + 1) * QUARTER)
            wg_ref[at, part] = master(chans.start).astype(bf16)
            wm_ref[at, part] = master(D_INNER + chans.start).astype(bf16)
        wm_ref[at, HALF:CHANS] = side[:, :SIDE].astype(bf16)
        dt_own = (lane % (HEADS // 2) // (LOCAL_HEADS // 2) == j) & (lane < HEADS)
        wm_ref[at, CHANS:MAIN] = jnp.where(dt_own, dt_cols, 0.0).astype(bf16)
    for k in range(D // HALF):
        wo_ref[:, k * HALF : (k + 1) * HALF] = dn_ref[k * out_rows : (k + 1) * out_rows, :].astype(bf16)

    greeted(EVERY_NEIGHBOUR)
    mains = WeightGather(copies, win_ref, own_rows, True)
    mains.swap(wm_ref)
    hids = GroupGather(copies, hid_ref, h_ref)
    copies.keep(cotv_ref, cotv_out)

    for k in range(HALF // LANES):
        lanes = slice(k * LANES, (k + 1) * LANES)
        chans_ref[1:2, lanes] = small_ref[own_row(NORM_ROW, k), :]
        for j in range(CONV + 1):
            taps_ref[j : j + 1, lanes] = small_ref[own_row(TAP_ROW + TAP_ROWS * j, k), :]
    for k in range(SIDE // LANES):
        lanes = slice(HALF + k * LANES, HALF + (k + 1) * LANES)
        for j in range(CONV + 1):
            row = TAP_ROW + TAP_ROWS * j + D_INNER // LANES + k
            taps_ref[j : j + 1, lanes] = small_ref[row : row + 1, :]
    head_row = jnp.broadcast_to(small_ref[HEAD_ROW : HEAD_ROW + 1, :], (TILE, LANES))
    next_row = jnp.broadcast_to(small_ref[HEAD_ROW + 1 : HEAD_ROW + 2, :], (TILE, LANES))
    a_log = pltpu.roll(head_row, LANES - HEADS, 1)
    lane8 = lax.broadcasted_iota(jnp.int32, (TILE, LANES), 1)
    spill = LANES - 2 * HEADS
    skip = jnp.where(lane8 < spill, pltpu.roll(head_row, spill, 1), pltpu.roll(next_row, spill, 1))
    own = lane8 < HEADS
    heads_ref[0:1, :] = head_lanes(jnp.where(own, head_row, 0.0))[0:1]
    heads_ref[1:2, :] = -jnp.exp(head_lanes(jnp.where(own, a_log, 0.0))[0:1])
    skip = head_lanes(jnp.where(own, skip, 0.0))[0:1]
    for q in range(PAIRS):
        chans_ref[0:1, q * LANES : (q + 1) * LANES] = own_pair(skip, 2 * q)

    def mark(c, _):
        rows = span_rows(c)
        seg = segc_ref[pl.ds(pl.multiple_of(c * SPAN, SPAN), SPAN + 2 * FRONT), :]
        here = seg[FRONT : FRONT + SPAN]
        last = seg[FRONT + SPAN - 1 : FRONT + SPAN]
        before = seg[FRONT - 1 : FRONT]
        cols = [seg[FRONT - RIM + k : FRONT - RIM + k + SPAN] == here for k in range(RIM)]
        cols += [seg[FRONT + RIM - k : FRONT + RIM - k + SPAN] == here for k in range(RIM)]
        cols += [here == last, here == before]
        lane_m = lax.broadcasted_iota(jnp.int32, (SPAN, TILE), 1)
        marks = jnp.zeros((SPAN, TILE), f32)
        for k, col in enumerate(cols):
            marks = jnp.where(lane_m == k, jnp.where(col, 1.0, 0.0), marks)
        marks_ref[rows, :] = marks
        carry_ref[pl.ds(c, 1), :] = jnp.broadcast_to(jnp.where(last == before, 1.0, 0.0), (1, LANES))
        return 0

    lax.fori_loop(0, spans, mark, 0)
    blocks = group_blocks()

    def norm(block):
        rows = block_rows(block, tokens)
        hid = h_ref[rows, :].astype(f32)
        scale = lax.rsqrt(jnp.sum(hid * hid, axis=1, keepdims=True) / D + norm_eps)
        for k in range(D // LANES):
            lanes = slice(k * LANES, (k + 1) * LANES)
            xn_ref[rows, lanes] = (h_ref[rows, lanes].astype(f32) * scale * small_ref[k : k + 1, :]).astype(bf16)

    mains.spread_swapped()
    copies.settle(hids.own)
    norm(blocks[0])
    gates = WeightGather(copies, wgate_ref, own_rows, True)
    gates.swap(wg_ref)
    hids.hand_on()
    norm(blocks[2])
    mains.hand_on()
    gates.spread_swapped()
    hids.finish()
    norm(blocks[1])
    norm(blocks[3])
    mains.hand_on_last()
    cots = GroupGather(copies, cotv_ref, back_ref)
    outs = WeightGather(copies, wout_ref, out_rows, False)
    outs.spread(wo_ref, ())
    outs_kept = copies.keep(wo_ref, outs.mine(()))
    mains.finish()
    copies.settle(mains.kept)

    def project(c, _):
        rows = span_rows(c)
        xn = xn_ref[rows, :]
        at = pl.ds(pl.multiple_of(FRONT + c * SPAN, FRONT), SPAN)
        for k in range(CHANS // 256):
            cols = slice(k * 256, (k + 1) * 256)
            convp_ref[at, cols] = dot(xn, win_ref[:, cols]).astype(bf16)
        dt_raw = dot(xn, win_ref[:, CHANS:MAIN]).astype(bf16).astype(f32)
        z = head_lanes(dt_raw) + heads_ref[0:1, :]
        z_ref[rows, :] = z
        small = jnp.exp(-jnp.abs(z))
        one_more = 1.0 + small
        is_one = one_more == 1.0
        log_more = jnp.where(is_one, small, jnp.log(one_more) * small / jnp.where(is_one, 1.0, one_more - 1.0))
        dt_ref[rows, :] = jnp.maximum(z, 0.0) + log_more
        return 0

    lax.fori_loop(0, spans, project, 0)
    rim = copies.send(convp_ref.at[pl.ds(rows_all, FRONT)], rim_ref, PART)
    gates.hand_on()
    s_ref[...] = jnp.zeros_like(s_ref)
    dgain_ref[...] = jnp.zeros_like(dgain_ref)

    def convolve(c, _):
        rows = span_rows(c)
        wide = pl.ds(pl.multiple_of(c * SPAN, SPAN), SPAN + FRONT)
        marks = marks_ref[rows, :]
        for k in range(CHANS // LANES):
            lanes = slice(k * LANES, (k + 1) * LANES)
            values = convp_ref[wide, lanes].astype(f32)
            total = taps_ref[CONV : CONV + 1, lanes] + taps_ref[RIM : RIM + 1, lanes] * values[FRONT:]
            for j in range(RIM):
                first = FRONT - RIM + j
                total = total + taps_ref[j : j + 1, lanes] * values[first : first + SPAN] * marks[:, j : j + 1]
            sig = 1.0 / (1.0 + jnp.exp(-total))
            value = (total * sig).astype(bf16)
            dtot_ref[rows, lanes] = sig * (1.0 + total * (1.0 - sig))
            if k < HALF // LANES:
                x_ref[rows, lanes] = value
            elif k == HALF // LANES:
                b_ref[rows, :] = value
            else:
                c_ref[rows, :] = value
        return 0

    lax.fori_loop(1, spans, convolve, 0)
    rim.wait_recv()
    convp_ref[0:FRONT, :] = jnp.where(p == 1, rim_ref[...].astype(f32), 0.0).astype(bf16)
    lax.fori_loop(0, 1, convolve, 0)
    gates.hand_on_last()

    def local_states(c, _):
        rows = span_rows(c)
        dt, cum = span_decay(dt_ref, heads_ref, c, 1)
        cum_ref[rows, :] = cum
        last = cum[SPAN - 1 : SPAN, :]
        end_weight = jnp.exp(last - cum) * dt * marks_ref[rows, 6:7]
        decay = jnp.exp(last) * carry_ref[pl.ds(c, 1), :]
        b = b_ref[rows, :]
        st_ref[c] = s_ref[...]
        for q in range(PAIRS):
            lanes = slice(q * LANES, (q + 1) * LANES)
            xw = (x_ref[rows, lanes].astype(f32) * own_pair(end_weight, 2 * q)).astype(bf16)
            s_ref[:, lanes] = s_ref[:, lanes] * own_pair(decay, 2 * q) + dot(b, xw, ((0,), (0,)))
        return 0

    lax.fori_loop(0, spans, local_states, 0)
    pass_ref[...] = s_ref[...].astype(bf16)
    state = copies.send(pass_ref, got_ref, PART)
    cots.hand_on()
    outs.hand_on()

    def inside(c, _):
        rows = span_rows(c)
        cum = cum_ref[rows, :]
        back_log = jnp.transpose(cum - jnp.log(dt_ref[rows, :]))
        scores = dot(c_ref[rows, :], b_ref[rows, :], ((1,), (1,)))
        row = lax.broadcasted_iota(jnp.int32, (SPAN, SPAN), 0)
        col = lax.broadcasted_iota(jnp.int32, (SPAN, SPAN), 1)
        mask = (row >= col) & (segc_ref[pl.ds(pl.multiple_of(FRONT + c * SPAN, FRONT), SPAN), :] == segr_ref[pl.ds(c, 1), :])
        lane = lax.broadcasted_iota(jnp.int32, (SPAN, LANES), 1)
        for q in range(PAIRS):
            lanes = slice(q * LANES, (q + 1) * LANES)
            x = x_ref[rows, lanes]
            parts = []
            for h in (lane_of(2 * q), lane_of(2 * q + 1)):
                gap = cum[:, h : h + 1] - back_log[h : h + 1, :]
                weighted = scores * jnp.exp(jnp.where(mask, gap, -1e30))
                parts.append(dot(weighted.astype(bf16), x))
            y_ref[rows, lanes] = jnp.where(lane < HEADDIM, parts[0], parts[1])
        return 0

    lax.fori_loop(0, spans, inside, 0)
    state.wait_recv()
    s_ref[...] = got_ref[...].astype(f32) * p.astype(f32)

    def across_spans(c, _):
        rows = span_rows(c)
        cum = cum_ref[rows, :]
        decay = jnp.exp(cum[SPAN - 1 : SPAN, :]) * carry_ref[pl.ds(c, 1), :]
        gain = jnp.exp(cum) * marks_ref[rows, 7:8]
        cc = c_ref[rows, :]
        for q in range(PAIRS):
            lanes = slice(q * LANES, (q + 1) * LANES)
            entering = s_ref[:, lanes]
            full = st_ref[c, :, lanes] + entering
            st_ref[c, :, lanes] = full
            y_ref[rows, lanes] += dot(cc, full.astype(bf16)) * own_pair(gain, 2 * q)
            s_ref[:, lanes] = entering * own_pair(decay, 2 * q)
        return 0

    lax.fori_loop(0, spans, across_spans, 0)
    gates.finish()
    copies.settle(gates.kept)

    def put_stat(k, c, column):
        wide = jnp.transpose(jnp.broadcast_to(column, (SPAN, LANES)))
        stat_ref[k, :, span_rows(c)] = wide[0:TILE, :]

    def exchange(k):
        return [copies.send(stat_ref.at[k], stats_ref.at[k, i], flips) for i, flips in enumerate(HOPS[1:])]

    def get_stat(k, c):
        cols = span_rows(c)
        total = stat_ref[k, :, cols] + stats_ref[k, 0, :, cols] + stats_ref[k, 1, :, cols] + stats_ref[k, 2, :, cols]
        return jnp.transpose(jnp.broadcast_to(total[0:1, :], (LANES, SPAN)))[:, 0:1] / D_INNER

    def values(rows, lanes):
        y_b = (y_ref[rows, lanes] + chans_ref[0:1, lanes] * x_ref[rows, lanes].astype(f32)).astype(bf16).astype(f32)
        gate = gate_ref[rows, lanes]
        sig = 1.0 / (1.0 + jnp.exp(-gate))
        return y_b, gate, sig

    def gating(c, _):
        rows = span_rows(c)
        xn = xn_ref[rows, :]
        total = jnp.zeros((SPAN, 1), f32)
        for k in range(HALF // 256):
            lanes = slice(k * 256, (k + 1) * 256)
            gate_ref[rows, lanes] = dot(xn, wgate_ref[:, lanes])
            y_b, gate, sig = values(rows, lanes)
            gated = y_b * (gate * sig)
            gated_ref[rows, lanes] = gated
            total = total + jnp.sum(gated * gated, axis=1, keepdims=True)
        put_stat(0, c, total)
        return 0

    lax.fori_loop(0, spans, gating, 0)
    outs.hand_on_last()
    squares = exchange(0)
    cots.finish()
    copies.settle(cots.own)
    outs.finish()
    copies.settle(outs_kept)

    def pull_out(c, _):
        rows = span_rows(c)
        back = back_ref[rows, :]
        total = jnp.zeros((SPAN, 1), f32)
        for k in range(HALF // 256):
            lanes = slice(k * 256, (k + 1) * 256)
            d_normed = dot(back, wout_ref[lanes, :], ((1,), (1,)))
            dn_ref[rows, lanes] = d_normed
            total = total + jnp.sum(gated_ref[rows, lanes] * (d_normed * chans_ref[1:2, lanes]), axis=1, keepdims=True)
        put_stat(1, c, total)
        return 0

    lax.fori_loop(0, spans, pull_out, 0)
    for copy in squares:
        copy.wait_recv()
    dots = exchange(1)

    def push_out(c, _):
        rows = span_rows(c)
        scale = lax.rsqrt(get_stat(0, c) + norm_eps)
        for k in range(HALF // 256):
            lanes = slice(k * 256, (k + 1) * 256)
            scaled = gated_ref[rows, lanes] * scale
            normed_ref[rows, lanes] = (scaled * chans_ref[1:2, lanes]).astype(bf16)
            dgain_ref[0:1, lanes] += jnp.sum(scaled * dn_ref[rows, lanes], axis=0, keepdims=True)
        normed = normed_ref[rows, :]
        for k in range(D // 256):
            cols = slice(k * 256, (k + 1) * 256)
            mix_ref[rows, cols] = dot(normed, wout_ref[:, cols]).astype(bf16)
        return 0

    copies.drain()
    lax.fori_loop(0, spans, push_out, 0)
    mixes = GroupScatter(copies, mix_ref, mix_bufs)
    mixes.to_t0(3)
    mixes.to_t0(1)
    for q in range(2):
        normed = normed_ref[:, q * HALF // 2 : (q + 1) * HALF // 2]
        for k in range(D // 512):
            cols = slice(k * 512, (k + 1) * 512)
            wout_ref[q * HALF // 2 : (q + 1) * HALF // 2, cols] = dot(normed, back_ref[:, cols], ((0,), (0,))).astype(bf16)
    go_halves = [wout_ref.at[pl.ds(pl.multiple_of(q * (HALF // 2), HALF // 2), HALF // 2)] for q in (1 - p, p)]
    g_out = GradientSum(copies, go_halves, out_rows, go_bufs, False)
    g_out.cores(0)
    g_out.cores(1)
    for copy in dots:
        copy.wait_recv()

    def back_gate(c, _):
        rows = span_rows(c)
        scale = lax.rsqrt(get_stat(0, c) + norm_eps)
        pulled = get_stat(1, c) * (scale * scale * scale)
        for k in range(HALF // LANES):
            lanes = slice(k * LANES, (k + 1) * LANES)
            y_b, gate, sig = values(rows, lanes)
            d_gated = scale * (dn_ref[rows, lanes] * chans_ref[1:2, lanes]) - gated_ref[rows, lanes] * pulled
            dy_ref[rows, lanes] = (d_gated * (gate * sig)).astype(bf16)
            dgate_ref[rows, lanes] = (d_gated * y_b * (sig * (1.0 + gate * (1.0 - sig)))).astype(bf16)
        return 0

    lax.fori_loop(0, spans, back_gate, 0)
    g_out.to_sides(0)
    s_ref[...] = jnp.zeros_like(s_ref)
    hsum_ref[...] = jnp.zeros_like(hsum_ref)
    dskip_ref[...] = jnp.zeros_like(dskip_ref)
    dtaps_ref[...] = jnp.zeros_like(dtaps_ref)

    def local_states(step, _):
        c = spans - 1 - step
        rows = span_rows(c)
        cum = cum_ref[rows, :]
        decay = jnp.exp(cum[SPAN - 1 : SPAN, :]) * carry_ref[pl.ds(c, 1), :]
        gain = jnp.exp(cum) * marks_ref[rows, 7:8]
        cc = c_ref[rows, :]
        for q in range(PAIRS):
            lanes = slice(q * LANES, (q + 1) * LANES)
            dyg = (dy_ref[rows, lanes].astype(f32) * own_pair(gain, 2 * q)).astype(bf16)
            dyg_ref[rows, lanes] = dyg
            ds = s_ref[:, lanes]
            dn_ref[pl.ds(pl.multiple_of(c * STATE, STATE), STATE), lanes] = ds
            s_ref[:, lanes] = ds * own_pair(decay, 2 * q) + dot(cc, dyg, ((0,), (0,)))
        return 0

    lax.fori_loop(0, spans, local_states, 0)
    passb_ref[...] = s_ref[...].astype(bf16)
    state = copies.send(passb_ref, gotb_ref, PART)

    width = D // 4
    gg_halves = [back_ref.at[:, pl.ds(k * HALF, HALF)] for k in range(2)]
    g_gate = GradientSum(copies, gg_halves, own_rows, gg_bufs, True)

    def gate_gradient(far):
        for half in range(2):
            first = pl.multiple_of(((1 - p if far else p) * 2 + half) * width, width)
            piece = dot(xn_ref[:, pl.ds(first, width)], dgate_ref[...], ((0,), (0,)))
            gg_halves[0 if far else 1][half * width : (half + 1) * width, :] = piece.astype(bf16)

    gate_gradient(True)
    g_gate.cores(0)
    gate_gradient(False)
    g_gate.cores(1)
    g_gate.to_sides(0)
    g_out.to_part()
    g_out.to_sides(1)
    g_gate.to_sides(1)

    def inside(c, _):
        rows = span_rows(c)
        cum = cum_ref[rows, :]
        fore_log = jnp.transpose(cum)
        back_log = cum - jnp.log(dt_ref[rows, :])
        b = b_ref[rows, :]
        cc = c_ref[rows, :]
        scores = dot(b, cc, ((1,), (1,)))
        row = lax.broadcasted_iota(jnp.int32, (SPAN, SPAN), 0)
        col = lax.broadcasted_iota(jnp.int32, (SPAN, SPAN), 1)
        mask = (col >= row) & (segc_ref[pl.ds(pl.multiple_of(FRONT + c * SPAN, FRONT), SPAN), :] == segr_ref[pl.ds(c, 1), :])
        lane = lax.broadcasted_iota(jnp.int32, (SPAN, LANES), 1)
        d_scores = jnp.zeros((SPAN, SPAN), f32)
        dc = jnp.zeros((SPAN, STATE), f32)
        for q in range(PAIRS):
            lanes = slice(q * LANES, (q + 1) * LANES)
            x = x_ref[rows, lanes]
            dy = dy_ref[rows, lanes]
            xf = x.astype(f32)
            parts = []
            for k in range(2):
                h = lane_of(2 * q + k)
                gap = fore_log[h : h + 1, :] - back_log[:, h : h + 1]
                decay_mat = jnp.exp(jnp.where(mask, gap, -1e30))
                parts.append(dot((scores * decay_mat).astype(bf16), dy))
                own = (lane < HEADDIM) if k == 0 else (lane >= HEADDIM)
                d_weights = dot(jnp.where(own, xf, 0.0).astype(bf16), dy, ((1,), (1,)))
                d_scores = d_scores + d_weights * decay_mat
            dxi_ref[rows, lanes] = jnp.where(lane < HEADDIM, parts[0], parts[1])
            dc = dc + dot(dyg_ref[rows, lanes], st_ref[c, :, lanes].astype(bf16), ((1,), (1,)))
            dskip_ref[0:1, lanes] += jnp.sum(dy.astype(f32) * xf, axis=0, keepdims=True)
        d_scores_b = d_scores.astype(bf16)
        dn_ref[side_at(c, 0)] = dot(d_scores_b, cc)
        dn_ref[side_at(c, 1)] = dc + dot(d_scores_b, b, ((0,), (0,)))
        return 0

    lax.fori_loop(0, spans, inside, 0)
    mixes.to_t1()
    state.wait_recv()
    s_ref[...] = gotb_ref[...].astype(f32) * (1 - p).astype(f32)

    def across_spans(step, _):
        c = spans - 1 - step
        rows = span_rows(c)
        dt = dt_ref[rows, :]
        cum = cum_ref[rows, :]
        last = cum[SPAN - 1 : SPAN, :]
        end_weight = jnp.exp(last - cum) * dt * marks_ref[rows, 6:7]
        decay = jnp.exp(last) * carry_ref[pl.ds(c, 1), :]
        b = b_ref[rows, :]
        db = dn_ref[side_at(c, 0)]
        edges = []
        for q in range(PAIRS):
            lanes = slice(q * LANES, (q + 1) * LANES)
            xf = x_ref[rows, lanes].astype(f32)
            dyf = dy_ref[rows, lanes].astype(f32)
            ew = own_pair(end_weight, 2 * q)
            dec = own_pair(decay, 2 * q)
            entering = s_ref[:, lanes]
            ds = dn_ref[pl.ds(pl.multiple_of(c * STATE, STATE), STATE), lanes] + entering
            s_ref[:, lanes] = entering * dec
            ds_b = ds.astype(bf16)
            db = db + dot((xf * ew).astype(bf16), ds_b, ((1,), (1,)))
            dx_state = dot(b, ds_b) * ew
            dx = dxi_ref[rows, lanes] + dx_state
            edges.append(
                jnp.sum(ds * st_ref[c, :, lanes], axis=0, keepdims=True) * dec
                + jnp.sum(dx_state * xf, axis=0, keepdims=True)
            )
            prod_ref[0:SPAN, lanes] = dyf * y_ref[rows, lanes]
            prod_ref[SPAN : 2 * SPAN, lanes] = xf * dx
            d_x = (dx + dyf * chans_ref[0:1, lanes]).astype(bf16).astype(f32)
            dtot_ref[rows, lanes] = d_x * dtot_ref[rows, lanes]
        dtot_ref[rows, HALF : HALF + STATE] = db * dtot_ref[rows, HALF : HALF + STATE]
        dtot_ref[rows, HALF + STATE :] = dn_ref[side_at(c, 1)] * dtot_ref[rows, HALF + STATE :]
        sums = own_sums(prod_ref[0 : 2 * SPAN, :])
        out_sum, in_sum = sums[:SPAN], sums[SPAN:]
        edge_sum = own_sums(jnp.broadcast_to(jnp.concatenate(edges, axis=1), (TILE, HALF)))[0:1]
        at_last = lax.broadcasted_iota(jnp.int32, (SPAN, LANES), 0) == SPAN - 1
        d_cum = out_sum - in_sum + jnp.where(at_last, edge_sum, 0.0)
        row = lax.broadcasted_iota(jnp.int32, (SPAN, SPAN), 0)
        col = lax.broadcasted_iota(jnp.int32, (SPAN, SPAN), 1)
        d_log = dot((col >= row).astype(f32), d_cum, precision=exact_prec)
        z = z_ref[rows, :]
        small = jnp.exp(-jnp.abs(z))
        sig = jnp.where(z >= 0.0, 1.0, small) / (1.0 + small)
        ratio = jnp.where(dt > 1e-30, sig / jnp.maximum(dt, 1e-30), 1.0)
        d_dt = d_log * heads_ref[1:2, :] * sig + in_sum * ratio
        hsum_ref[0:1, :] += jnp.sum(d_log * dt, axis=0, keepdims=True)
        hsum_ref[1:2, :] += jnp.sum(d_dt, axis=0, keepdims=True)
        dmain_ref[rows, CHANS:MAIN] = head_lanes(d_dt, back=True).astype(bf16)
        return 0

    lax.fori_loop(0, spans, across_spans, 0)
    rims_ref[...] = dtot_ref[0:TILE, :]
    rim = copies.send(rims_ref, rimr_ref, PART)
    g_gate.to_part()

    def convolve(c, _):
        rows = span_rows(c)
        marks = marks_ref[rows, :]
        fore = pl.ds(pl.multiple_of(c * SPAN, SPAN), SPAN + FRONT)
        hind = pl.ds(pl.multiple_of(c * SPAN, SPAN), SPAN + TILE)
        for k in range(CHANS // LANES):
            lanes = slice(k * LANES, (k + 1) * LANES)
            later = dtot_ref[hind, lanes]
            earlier = convp_ref[fore, lanes].astype(f32)
            own = later[0:SPAN]
            d_conv = taps_ref[RIM : RIM + 1, lanes] * own
            dtaps_ref[RIM : RIM + 1, lanes] += jnp.sum(own * earlier[FRONT:], axis=0, keepdims=True)
            dtaps_ref[CONV : CONV + 1, lanes] += jnp.sum(own, axis=0, keepdims=True)
            for j in range(RIM):
                ahead = RIM - j
                d_conv = d_conv + taps_ref[j : j + 1, lanes] * later[ahead : ahead + SPAN] * marks[:, 3 + j : 4 + j]
                first = FRONT - ahead
                dtaps_ref[j : j + 1, lanes] += jnp.sum(
                    own * earlier[first : first + SPAN] * marks[:, j : j + 1], axis=0, keepdims=True
                )
            dmain_ref[rows, lanes] = d_conv.astype(bf16)
        return 0

    lax.fori_loop(0, spans - 1, convolve, 0)
    rim.wait_recv()
    dtot_ref[pl.ds(spans * SPAN, TILE), :] = jnp.where(p == 0, rimr_ref[...], 0.0)
    lax.fori_loop(spans - 1, spans, convolve, 0)

    mixes.left()
    dpre_ref[...] = jnp.zeros_like(dpre_ref)

    def token_grad(block, keep):
        rows = block_rows(block, tokens)
        d_main = dmain_ref[rows, :]
        d_gate = dgate_ref[rows, :]
        hid = h_ref[rows, :].astype(f32)
        scale = lax.rsqrt(jnp.sum(hid * hid, axis=1, keepdims=True) / D + norm_eps)
        for k in range(D // 256):
            cols = slice(k * 256, (k + 1) * 256)
            part = dot(d_main, win_ref[cols, :], ((1,), (1,))) + dot(d_gate, wgate_ref[cols, :], ((1,), (1,)))
            dpre_ref[0:1, cols] += jnp.sum(h_ref[rows, cols].astype(f32) * scale * part, axis=0, keepdims=True)
            if keep:
                first = k * 256 // HALF * tokens
                y_ref[first : first + tokens, k * 256 % HALF : k * 256 % HALF + 256] = part
            else:
                mix_ref[rows, cols] = part.astype(bf16)

    def store_gate(i, value):
        kept = pl.ds(2 * SPAN + i * own_rows, own_rows)
        gate_ref[kept, :] = value
        copies.keep(gate_ref.at[kept], ggate_out.at[blocks[i][0], blocks[i][1]])

    def store_main(i, value):
        for first, count in ((0, HALF), (HALF, MAIN - HALF)):
            kept = pl.ds((first // HALF * TP + i) * own_rows, own_rows)
            gated_ref[kept, 0:count] = value[:, first : first + count]
            copies.keep(
                gated_ref.at[kept, pl.ds(0, count)], gmain_out.at[blocks[i][0], blocks[i][1], :, pl.ds(first, count)]
            )

    total = g_out.total(0)
    for k in range(D // HALF):
        kept = pl.ds(2 * TP * own_rows + k * out_rows, out_rows)
        gated_ref[kept, :] = total[:, k * HALF : (k + 1) * HALF]
        copies.keep(gated_ref.at[kept], gout_out.at[:, pl.ds(k * HALF, HALF)])
    g_out.left()
    gm_halves = [wout_ref.at[:, pl.ds(0, MAIN)], gm_ref]

    def grad_half(far):
        part = 1 - p if far else p
        out = gm_halves[0 if far else 1]

        def piece(i, _):
            xn = xn_ref[:, pl.ds(pl.multiple_of((part * 2 + i) * width, width), width)]
            rows = pl.ds(pl.multiple_of(i * width, width), width)
            for k in range(MAIN // 384):
                cols = slice(k * 384, (k + 1) * 384)
                out[rows, cols] = dot(xn, dmain_ref[:, cols], ((0,), (0,))).astype(bf16)
            return 0

        lax.fori_loop(0, 2, piece, 0)

    grad_half(True)
    g_main = GradientSum(copies, gm_halves, own_rows, gm_bufs, True)
    g_main.cores(0)
    dxs = GroupScatter(copies, mix_ref, dx_bufs)
    token_grad(blocks[3], False)
    dxs.to_t0(3)
    g_main.to_sides(0)
    token_grad(blocks[1], False)
    dxs.to_t0(1)
    grad_half(False)
    g_main.cores(1)
    g_main.to_part((1,))
    g_gate.to_group(store_gate)
    g_main.to_part((2,))
    g_main.to_sides(1)
    g_main.to_part((3,))

    mixer = mix_ref[mixes.block(0), :].astype(f32) + mixes.finish()
    copies.left([mixes.last_copy])
    for k in range(D // HALF):
        kept = pl.ds(spans * STATE + k * tokens, tokens)
        dn_ref[kept, :] = mixer[:, k * HALF : (k + 1) * HALF]
        copies.keep(dn_ref.at[kept], mixer_out.at[:, pl.ds(k * HALF, HALF)])
    hid = h_ref[mixes.block(0), :].astype(f32)
    valid = valid_ref[...]
    counts = [jnp.sum(valid * jnp.sum(v * v, axis=1, keepdims=True), axis=0, keepdims=True) for v in (hid, mixer)]
    counts.append(jnp.sum(valid, axis=0, keepdims=True))
    scalars = jnp.zeros((1, LANES), f32)
    for k in range(3):
        scalars = jnp.where(lane == k, counts[k], scalars)
    box = box_ref.at[0]
    box[...] = jnp.zeros_like(box)
    box[OWN_SUMS : OWN_SUMS + 1, :] = scalars

    token_grad(blocks[2], False)
    g_main.to_part((0,))
    dxs.to_t1()
    token_grad(blocks[0], True)

    for k in range(D // LANES):
        box[k : k + 1, :] = dpre_ref[0:1, k * LANES : (k + 1) * LANES]
    for k in range(HALF // LANES):
        lanes = slice(k * LANES, (k + 1) * LANES)
        box[OWN_NORM + k : OWN_NORM + k + 1, :] = dgain_ref[0:1, lanes]
        for j in range(CONV + 1):
            row = OWN_TAP + j * (HALF // LANES) + k
            box[row : row + 1, :] = dtaps_ref[j : j + 1, lanes]
    for k in range(SIDE // LANES):
        lanes = slice(HALF + k * LANES, HALF + (k + 1) * LANES)
        for j in range(CONV + 1):
            row = OWN_SIDE + j * (SIDE // LANES) + k
            box[row : row + 1, :] = dtaps_ref[j : j + 1, lanes]
    hsum_ref[0:1, :] = hsum_ref[0:1, :] * heads_ref[1:2, :]
    hsum_ref[2:3, :] = own_sums(dskip_ref[...])[0:1, :]
    lane8 = lax.broadcasted_iota(jnp.int32, (TILE, LANES), 1)
    box[OWN_HEAD : OWN_HEAD + 3, :] = jnp.where(lane8 < HEADS, head_lanes(hsum_ref[...], back=True), 0.0)[0:3]

    def small_step(k, hops):
        return [copies.send(box_ref.at[k], boxes_ref.at[k, i], flips) for i, flips in enumerate(hops)]

    def small_add(k, sent):
        total = box_ref[k]
        for i, copy in enumerate(sent):
            copy.wait_recv()
            total = total + boxes_ref[k, i]
        box_ref[k + 1] = total

    small = small_step(0, (CORE, SIDEWAYS, SIDE_CORE))
    g_gate.finish(store_gate)
    small_add(0, small)
    small = small_step(1, (PART,))
    small_add(1, small)
    small = small_step(2, (T0, T1, DIAG))
    g_main.to_group(store_main)
    dx = dxs.finish()
    for k in range(D // HALF):
        kept = pl.ds(k * tokens, tokens)
        y_ref[kept, :] += dx[:, k * HALF : (k + 1) * HALF]
        copies.keep(y_ref.at[kept], dx_out.at[:, pl.ds(k * HALF, HALF)])
    small_add(2, small)
    total_ref[...] = jnp.zeros_like(total_ref)
    total_ref[0:NORM_ROW, :] = box_ref[3, 0:NORM_ROW]
    third = QUARTER // LANES
    runs = [(OWN_NORM, NORM_ROW)]
    runs += [(OWN_TAP + j * 2 * third, TAP_ROW + j * TAP_ROWS) for j in range(CONV + 1)]
    for i, block in enumerate(blocks):
        source = box_ref.at[2] if i == 0 else boxes_ref.at[2, i - 1]
        place_at = (block[0] * 2 + block[1]) * third
        for own, first in runs:
            for k in range(2 * third):
                row = first + k // third * (D_INNER // 2 // LANES) + place_at + k % third
                total_ref[pl.ds(row, 1), :] = source[own + k : own + k + 1, :]
    for j in range(CONV + 1):
        row, own = TAP_ROW + TAP_ROWS * j + D_INNER // LANES, OWN_SIDE + j * (SIDE // LANES)
        total_ref[row : row + SIDE // LANES, :] = box_ref[3, own : own + SIDE // LANES]
    d_rate, d_shift, d_skip = (
        jnp.broadcast_to(box_ref[3, OWN_HEAD + k : OWN_HEAD + k + 1], (TILE, LANES)) for k in range(3)
    )
    spill = LANES - 2 * HEADS
    joined = d_shift + pltpu.roll(d_rate, HEADS, 1) + jnp.where(lane8 >= 2 * HEADS, pltpu.roll(d_skip, 2 * HEADS, 1), 0.0)
    total_ref[HEAD_ROW : HEAD_ROW + 1, :] = joined[0:1]
    spilled = jnp.where(lane8 < HEADS - spill, pltpu.roll(d_skip, LANES - spill, 1), 0.0)
    total_ref[HEAD_ROW + 1 : HEAD_ROW + 2, :] = spilled[0:1]
    total_ref[SMALL_ROWS : SMALL_ROWS + 1, :] = box_ref[3, OWN_SUMS : OWN_SUMS + 1]
    g_main.finish(store_main)
    copies.drain()


def update_kernel(
    hid_ref, mixer_ref, dx_ref, back_ref, pre_ref, gmain_ref, ggate_ref, gout_ref, total_ref,
    inw_ref, inm_ref, inv_ref, outw_ref, outm_ref, outv_ref, small_ref, smallm_ref, smallv_ref,
    output_ref, gh_ref, inm_out, inv_out, inw_out, outm_out, outv_out, outw_out, smallm_out, smallv_out, smallw_out, rms_ref,
):
    hid = hid_ref[...].astype(f32)
    output_ref[...] = (hid + mixer_ref[...]).astype(bf16)
    scale = lax.rsqrt(jnp.sum(hid * hid, axis=1, keepdims=True) / D + norm_eps)
    d_pre = dx_ref[...] * pre_ref[...]
    pulled = jnp.sum(hid * d_pre, axis=1, keepdims=True) / D * (scale * scale * scale)
    gh_ref[...] = back_ref[...].astype(f32) + scale * d_pre - hid * pulled

    def update(refs, outs, cols, grad, rate=0.02, decay=0.1):
        weight, moment, second = (ref[:, cols] for ref in refs)
        for out, value in zip(outs, adamw(weight, moment, second, grad, rate, decay)):
            out[:, cols] = value

    every = slice(None)
    update((outw_ref, outm_ref, outv_ref), (outm_out, outv_out, outw_out), every, gout_ref[...])
    in_refs, in_outs = (inw_ref, inm_ref, inv_ref), (inm_out, inv_out, inw_out)
    for j in range(TP):
        for k, chans in enumerate(own_chans(j)):
            part = slice(k * QUARTER, (k + 1) * QUARTER)
            update(in_refs, in_outs, chans, ggate_ref[j // 2, j % 2, :, part])
            scan = slice(D_INNER + chans.start, D_INNER + chans.stop)
            update(in_refs, in_outs, scan, gmain_ref[j // 2, j % 2, :, part])
    rest_grad = gmain_ref[0, 0, :, HALF:] + gmain_ref[0, 1, :, HALF:] + gmain_ref[1, 0, :, HALF:] + gmain_ref[1, 1, :, HALF:]
    first = 2 * D_INNER
    update(in_refs, in_outs, slice(first, first + SIDE), rest_grad[:, :SIDE])
    update(in_refs, in_outs, slice(first + SIDE, first + SIDE + HEADS), rest_grad[:, SIDE : SIDE + HEADS])

    @pl.when(pl.program_id(0) == 0)
    def _():
        update(
            (small_ref, smallm_ref, smallv_ref), (smallm_out, smallv_out, smallw_out), every, total_ref[0:SMALL_ROWS, :], 0.2, 0.0
        )
        totals = total_ref[SMALL_ROWS:, :]
        rms_ref[...] = jnp.sqrt(totals / (totals[0:1, 2:3] * D))


def linked(kernel, name, collective_id, in_specs, outs, scratch):
    return pl.pallas_call(
        kernel,
        name=name,
        in_specs=in_specs,
        out_shape=tuple(o for o, _ in outs),
        out_specs=tuple(s for _, s in outs),
        scratch_shapes=scratch,
        compiler_params=pltpu.CompilerParams(
            collective_id=collective_id, has_side_effects=True, vmem_limit_bytes=VMEM_LIMIT
        ),
    )


def shards_linked(
    hidden, cotangent, segments, valid, in_w, in_m, in_v, out_w, out_m, out_v, small_w, small_m, small_v,
):
    part = lax.axis_index("part")
    own_rows, out_rows = in_w.shape[0], out_w.shape[0]
    tok_rows = hidden.shape[1]
    rows = tok_rows * TP
    spans = rows // SPAN
    edge = jnp.full((FRONT,), -1, jnp.int32)
    seg_wide = lax.dynamic_slice_in_dim(jnp.concatenate([edge, segments[0], edge]), part * rows, rows + 2 * FRONT)
    seg_spans = seg_wide[FRONT : FRONT + rows].reshape(spans, SPAN)
    valid_col = valid[0].astype(f32)[:, None]
    small_size = small_w.shape[0]

    def small_box(array):
        return jnp.pad(array, (0, SMALL_ROWS * LANES - small_size)).reshape(SMALL_ROWS, LANES)

    small_w, small_m, small_v = small_box(small_w), small_box(small_m), small_box(small_v)
    pre_row = small_w[:NORM_ROW].reshape(1, D)

    wide = (rows, D)
    half = (rows, HALF)
    lanes = (rows, LANES)
    side = (rows, STATE)
    state = (STATE, HALF)
    main_outs = (
        (shape((tok_rows, D), bf16), HBM),
        (shape((tok_rows, D), f32), HBM),
        (shape((2, 2, own_rows, HALF), f32), HBM),
        (shape((2, 2, own_rows, MAIN), f32), HBM),
        (shape((tok_rows, D), f32), HBM),
        (shape((out_rows, D), f32), HBM),
        (shape((BOX_ROWS, LANES), f32), VMEM),
    )
    main_scratch = (
        (wide, bf16),
        (wide, bf16),
        ((D, MAIN), bf16),
        ((rows + FRONT, CHANS), bf16),
        (half, bf16),
        (side, bf16),
        (side, bf16),
        ((rows + FRONT, CHANS), f32),
        (lanes, f32),
        (lanes, f32),
        (lanes, f32),
        (half, f32),
        ((spans, *state), f32),
        ((D, HALF), bf16),
        ((HALF, D), bf16),
        (wide, bf16),
        (half, bf16),
        (wide, bf16),
        (half, bf16),
        (half, bf16),
        ((rows, MAIN), bf16),
        ((TILE, HALF), f32),
        ((TILE, CHANS), f32),
        ((TILE, LANES), f32),
        ((TILE, HALF), f32),
        ((rows, TILE), f32),
        ((spans, LANES), f32),
        (state, f32),
        (state, bf16),
        (state, bf16),
        ((FRONT, CHANS), bf16),
        (half, f32),
        (half, f32),
        (half, f32),
        ((2, TILE, rows), f32),
        ((2, 3, TILE, rows), f32),
        (half, bf16),
        (state, bf16),
        (state, bf16),
        ((TILE, CHANS), f32),
        ((TILE, CHANS), f32),
        ((TILE, LANES), f32),
        ((TILE, HALF), f32),
        ((TILE, CHANS), f32),
        ((TILE, D), f32),
        ((4, OWN_ROWS, LANES), f32),
        ((3, 3, OWN_ROWS, LANES), f32),
        ((D // 2, MAIN), bf16),
    )
    back_own, mixer, g_gate, g_main, d_x_normed, g_out, totals = linked(
        functools.partial(main_kernel, spans), "main", 1, [*[HBM] * 4, *[VMEM] * 5], main_outs,
        [
            *[pltpu.VMEM(dims, dtype) for dims, dtype in main_scratch],
            *sum_buffers(out_rows, D, False),
            *sum_buffers(own_rows, HALF, True),
            *sum_buffers(own_rows, MAIN, True),
            *scatter_buffers(tok_rows),
            *scatter_buffers(tok_rows),
            *sems(200, 48),
        ],
    )(hidden[0], in_w, out_w, cotangent[0], in_w[:, 2 * D_INNER :], valid_col, small_w, seg_wide[:, None], seg_spans)

    steps = own_rows // TILE

    def cut(dims, axis=0):
        block = tuple(size // steps if k == axis else size for k, size in enumerate(dims))
        return pl.BlockSpec(block, lambda i: tuple(i if k == axis else 0 for k in range(len(dims))))

    def fixed(dims):
        return pl.BlockSpec(dims, lambda i: (0, 0))

    tokens, matrix_in, matrix_out, small_dims = (tok_rows, D), in_w.shape, out_w.shape, (SMALL_ROWS, LANES)
    out_dims = [tokens] * 2 + [matrix_in] * 3 + [matrix_out] * 3
    (
        output, grad_hidden, in_m_new, in_v_new, in_w_new, out_m_new, out_v_new, out_w_new,
        small_m_new, small_v_new, small_w_new, rms,
    ) = pl.pallas_call(
        update_kernel,
        name="update",
        grid=(steps,),
        in_specs=[
            *[cut(tokens)] * 4,
            fixed((1, D)),
            cut(g_main.shape, 2),
            cut(g_gate.shape, 2),
            cut(matrix_out),
            fixed((BOX_ROWS, LANES)),
            *[cut(matrix_in)] * 3,
            *[cut(matrix_out)] * 3,
            *[fixed(small_dims)] * 3,
        ],
        out_shape=[
            *[shape(dims, bf16 if k == 0 else f32) for k, dims in enumerate(out_dims)],
            *[shape(small_dims, f32)] * 3,
            shape((TILE, LANES), f32),
        ],
        out_specs=[*[cut(dims) for dims in out_dims], *[fixed(small_dims)] * 3, fixed((TILE, LANES))],
        compiler_params=pltpu.CompilerParams(vmem_limit_bytes=VMEM_LIMIT),
    )(
        hidden[0], mixer, d_x_normed, back_own, pre_row, g_main, g_gate, g_out, totals,
        in_w, in_m, in_v, out_w, out_m, out_v, small_w, small_m, small_v,
    )
    small_m_new, small_v_new, small_w_new = (
        array.reshape(-1)[:small_size] for array in (small_m_new, small_v_new, small_w_new)
    )
    return (
        output[None], grad_hidden[None], in_m_new, in_v_new, in_w_new, out_m_new, out_v_new, out_w_new,
        small_m_new, small_v_new, small_w_new, rms[0, :2],
    )


def solution(mesh):
    seq, wt = mesh.shape["seq"], mesh.shape["wt"]
    split = Mesh(mesh.devices.reshape(seq // TP, 2, 2, wt // 2, 2), EVERYONE)
    streams = ("w1", "w0")
    tokens = ("part", "t1", "t0")
    matrix = P(EVERYONE, None)
    stream = P(streams, tokens, None)
    size = mesh.devices.size
    fits = seq == 2 * TP and wt == 4 and D // size % 16 == 0 and D_INNER // size % 16 == 0
    return jax.shard_map(
        shards_linked if fits else shards_general,
        mesh=split,
        in_specs=(
            stream, stream, P(streams, None), P(streams, tokens), matrix, matrix, matrix, matrix, matrix, matrix, P(), P(), P(),
        ),
        out_specs=(stream, stream, matrix, matrix, matrix, matrix, matrix, matrix, P(), P(), P(), P()),
        check_vma=False,
    )
```

profile of v0, /device:TPU:0, one launch (start us, length us, event | category | flops | bytes accessed | tf_op | source)
XLA Modules:
  0.0 204.7 jit_solution(365849641439174386)
XLA Ops:
  0.6 0.7 convert_bitcast_fusion
  1.3 0.7 reduce
  2.1 0.1 concatenate.3
  2.1 0.1 dynamic_slice.3
  2.2 0.1 slice.24
  2.3 0.6 reshape.62.segr_ref
  2.9 0.7 slice.25
  3.6 0.6 reshape.63.pre_ref
  4.2 1.5 slice.23.inside_ref
  5.7 1.5 pad_bitcast_fusion.2.small_ref
  7.2 0.8 copy.25.valid_ref
  8.0 1.6 pad_bitcast_fusion
  9.6 0.9 broadcast_in_dim.13.segc_ref
  10.6 183.4 %main.1 = (bf16[192,1536]{1,0:T(8,128)(2,1)}, f32[192,1536]{1,0:T(8,128)}, f32[2,2,48,768]{3,2,1,0:T(8,128)}, f32[2,2,48,1152]{3,2,1,0:T(8,128)}, f32[192,1536]{...) custom-call(bf16[192,1536]{1,0:T(8,128)(2,1)} %bitcast.20, f32[48,6448]{1,0:T(8,128)} %inw_ref.1, ...), custom_call_target="tpu_custom_call" | custom-call | tf_op jit(solution)/shard_map/main/pallas_call | solution.py:1673
  194.0 9.5 %update.1 = (bf16[192,1536]{1,0:T(8,128)(2,1)}, f32[192,1536]{1,0:T(8,128)}, f32[48,6448]{1,0:T(8,128)}, f32[48,6448]{1,0:T(8,128)}, f32[48,6448]{1,0:T(8,128)},...) custom-call(bf16[192,1536]{1,0:T(8,128)(2,1)} %bitcast.21, ...), custom_call_target="tpu_custom_call" | custom-call | tf_op jit(solution)/shard_map/update/pallas_call | solution.py:1700
  203.5 1.2 slice_bitcast_fusion
  (1 shorter events, 0.0 us)
where the time goes:
time: 205 us
  Pallas kernels  193 us (94%)
  local copies, waits for them, and re-layouts  9.69 us (5%)
    pallas_call x1, Pallas kernels, shards_linked(): linked(functools.partial(main_kernel, spans), 'main', 1, [*[HBM] * 4, *[V...  183 us
    pallas_call x1, Pallas kernels, shards_linked(): pl.pallas_call(update_kernel, name='update', grid=(steps,), in_specs=[*[c...  9.54 us

commit v1 on v0

--- a/solution.py
+++ b/solution.py
@@ -605,11 +605,17 @@
         self.rows = src.shape[0]
         self.halves = (0, self.rows // 2)
         own = group_blocks()[0]
-        self.own = copies.keep(src, self.at(own, 0, self.rows))
-        size = self.rows // 2
-        self.along_t1 = [copies.send(src.at[pl.ds(h, size)], self.at(own, h, size), T1) for h in self.halves]
-        self.along_t0 = [copies.send(src.at[pl.ds(h, size)], self.at(own, h, size), T0) for h in self.halves]
-        self.diagonal = []
+        self.src, self.own, self.size = src, copies.keep(src, self.at(own, 0, self.rows)), self.rows // 2
+        self.along_t1, self.along_t0, self.diagonal = self.start(T1), [], []
+
+    def start(self, flips):
+        own = group_blocks()[0]
+        return [
+            self.copies.send(self.src.at[pl.ds(h, self.size)], self.at(own, h, self.size), flips) for h in self.halves
+        ]
+
+    def start_t0(self):
+        self.along_t0 = self.start(T0)
 
     def at(self, block, first, size):
         return self.dst.at[pl.ds(pl.multiple_of((block[0] * 2 + block[1]) * self.rows + first, size), size)]
@@ -848,13 +854,13 @@
 
 
 def main_kernel(
-    spans, hid_ref, inw_hbm, outw_hbm, cot_hbm, inside_ref, valid_ref, small_ref, segc_ref, segr_ref,
+    spans, hid_ref, inw_hbm, outw_hbm, cot_hbm, inside_ref, valid_ref, small_ref, segs_ref,
     cotv_out, mixer_out, ggate_out, gmain_out, dx_out, gout_out, total_ref,
     h_ref, xn_ref, win_ref, convp_ref, x_ref, b_ref, c_ref, dtot_ref, dt_ref, z_ref, cum_ref, y_ref, st_ref,
     wgate_ref, wout_ref, back_ref, normed_ref, mix_ref, dy_ref, dgate_ref, dmain_ref, dgain_ref, taps_ref, heads_ref, chans_ref,
     marks_ref, carry_ref, s_ref, pass_ref, got_ref, rim_ref, gated_ref, gate_ref, dn_ref,
     stat_ref, stats_ref, dyg_ref, passb_ref, gotb_ref, rims_ref, rimr_ref, hsum_ref, dskip_ref, dtaps_ref,
-    dpre_ref, box_ref, boxes_ref, gm_ref,
+    dpre_ref, box_ref, boxes_ref, gm_ref, segc_ref, segr_ref, validc_ref,
     *rest,
 ):
     go_bufs, gg_bufs, gm_bufs, mix_bufs, dx_bufs = rest[:3], rest[3:7], rest[7:11], rest[11:14], rest[14:17]
@@ -885,11 +891,27 @@
     ]
     loads.append(copies.keep(cot_hbm, cotv_ref))
 
-    side = inside_ref[...]
+    def column(row):
+        return jnp.transpose(jnp.broadcast_to(row, (LANES, SPAN)))[:, 0:1]
+
+    for c in range(spans):
+        row = segs_ref[0:1, pl.ds(pl.multiple_of(p * rows_all + c * SPAN, LANES), SPAN)].astype(f32)
+        segr_ref[c : c + 1, :] = row
+        segc_ref[FRONT + c * SPAN : FRONT + (c + 1) * SPAN, :] = column(row)
+    around = rows_all - SPAN
+    row = segs_ref[0:1, pl.ds(pl.multiple_of(p * around, LANES), SPAN)].astype(f32)
+    segc_ref[0:FRONT, :] = jnp.where(p == 1, column(row)[SPAN - FRONT :], -1.0)
+    row = segs_ref[0:1, pl.ds(pl.multiple_of(rows_all + p * around, LANES), SPAN)].astype(f32)
+    segc_ref[FRONT + rows_all :, :] = jnp.where(p == 0, column(row)[0:FRONT], -1.0)
+    stat_ref[0] = jnp.zeros_like(stat_ref[0])
+    stat_ref[0, 0:1, 0:tokens] = valid_ref[...].astype(f32)
+    validc_ref[...] = column(stat_ref[0, 0:1, 0:SPAN])[0:tokens]
+
+    side = inside_ref[:, 0 : SIDE + HEADS]
     dt_cols = jnp.concatenate([side[:, SIDE:], jnp.zeros((own_rows, LANES - HEADS), f32)], axis=1)
     for copy in loads:
         copies.settle(copy)
-    cotv_ref[...] = (cotv_ref[...].astype(f32) * valid_ref[...]).astype(bf16)
+    cotv_ref[...] = (cotv_ref[...].astype(f32) * validc_ref[...]).astype(bf16)
 
     def master(first):
         return gate_ref[first // HALF * own_rows : (first // HALF + 1) * own_rows, first % HALF : first % HALF + QUARTER]
@@ -910,6 +932,7 @@
     mains = WeightGather(copies, win_ref, own_rows, True)
     mains.swap(wm_ref)
     hids = GroupGather(copies, hid_ref, h_ref)
+    hids.start_t0()
     copies.keep(cotv_ref, cotv_out)
 
     for k in range(HALF // LANES):
@@ -935,24 +958,23 @@
     for q in range(PAIRS):
         chans_ref[0:1, q * LANES : (q + 1) * LANES] = own_pair(skip, 2 * q)
 
-    def mark(c, _):
-        rows = span_rows(c)
-        seg = segc_ref[pl.ds(pl.multiple_of(c * SPAN, SPAN), SPAN + 2 * FRONT), :]
-        here = seg[FRONT : FRONT + SPAN]
-        last = seg[FRONT + SPAN - 1 : FRONT + SPAN]
+    def mark(first, count):
+        seg = segc_ref[pl.ds(first, FRONT + count), :]
+        here = seg[FRONT:]
+        last = seg[FRONT + count - 1 :]
         before = seg[FRONT - 1 : FRONT]
-        cols = [seg[FRONT - RIM + k : FRONT - RIM + k + SPAN] == here for k in range(RIM)]
-        cols += [seg[FRONT + RIM - k : FRONT + RIM - k + SPAN] == here for k in range(RIM)]
-        cols += [here == last, here == before]
-        lane_m = lax.broadcasted_iota(jnp.int32, (SPAN, TILE), 1)
-        marks = jnp.zeros((SPAN, TILE), f32)
-        for k, col in enumerate(cols):
+        cols = {k: seg[FRONT - RIM + k : FRONT - RIM + k + count] == here for k in range(RIM)}
+        cols[6], cols[7] = here == last, here == before
+        lane_m = lax.broadcasted_iota(jnp.int32, (count, TILE), 1)
+        marks = jnp.zeros((count, TILE), f32)
+        for k, col in cols.items():
             marks = jnp.where(lane_m == k, jnp.where(col, 1.0, 0.0), marks)
-        marks_ref[rows, :] = marks
-        carry_ref[pl.ds(c, 1), :] = jnp.broadcast_to(jnp.where(last == before, 1.0, 0.0), (1, LANES))
-        return 0
-
-    lax.fori_loop(0, spans, mark, 0)
+        marks_ref[pl.ds(first, count), :] = marks
+        return jnp.broadcast_to(jnp.where(last == before, 1.0, 0.0), (1, LANES))
+
+    for c in range(spans):
+        carry_ref[c : c + 1, :] = mark(c * SPAN, SPAN)
+    mark(rows_all, TILE)
     blocks = group_blocks()
 
     def norm(block):
@@ -973,10 +995,11 @@
     mains.hand_on()
     gates.spread_swapped()
     hids.finish()
+    cots = GroupGather(copies, cotv_ref, back_ref)
+    cots.start_t0()
     norm(blocks[1])
     norm(blocks[3])
     mains.hand_on_last()
-    cots = GroupGather(copies, cotv_ref, back_ref)
     outs = WeightGather(copies, wout_ref, out_rows, False)
     outs.spread(wo_ref, ())
     outs_kept = copies.keep(wo_ref, outs.mine(()))
@@ -1009,14 +1032,14 @@
     def convolve(c, _):
         rows = span_rows(c)
         wide = pl.ds(pl.multiple_of(c * SPAN, SPAN), SPAN + FRONT)
-        marks = marks_ref[rows, :]
+        masks = [jnp.broadcast_to(marks_ref[rows, j : j + 1], (SPAN, LANES)) for j in range(RIM)]
         for k in range(CHANS // LANES):
             lanes = slice(k * LANES, (k + 1) * LANES)
             values = convp_ref[wide, lanes].astype(f32)
             total = taps_ref[CONV : CONV + 1, lanes] + taps_ref[RIM : RIM + 1, lanes] * values[FRONT:]
             for j in range(RIM):
                 first = FRONT - RIM + j
-                total = total + taps_ref[j : j + 1, lanes] * values[first : first + SPAN] * marks[:, j : j + 1]
+                total = total + taps_ref[j : j + 1, lanes] * values[first : first + SPAN] * masks[j]
             sig = 1.0 / (1.0 + jnp.exp(-total))
             value = (total * sig).astype(bf16)
             dtot_ref[rows, lanes] = sig * (1.0 + total * (1.0 - sig))
@@ -1045,8 +1068,9 @@
         st_ref[c] = s_ref[...]
         for q in range(PAIRS):
             lanes = slice(q * LANES, (q + 1) * LANES)
-            xw = (x_ref[rows, lanes].astype(f32) * own_pair(end_weight, 2 * q)).astype(bf16)
-            s_ref[:, lanes] = s_ref[:, lanes] * own_pair(decay, 2 * q) + dot(b, xw, ((0,), (0,)))
+            dyg_ref[rows, lanes] = (x_ref[rows, lanes].astype(f32) * own_pair(end_weight, 2 * q)).astype(bf16)
+            s_ref[:, lanes] = s_ref[:, lanes] * own_pair(decay, 2 * q)
+        s_ref[...] += dot(b, dyg_ref[rows, :], ((0,), (0,)))
         return 0
 
     lax.fori_loop(0, spans, local_states, 0)
@@ -1218,7 +1242,8 @@
             dyg_ref[rows, lanes] = dyg
             ds = s_ref[:, lanes]
             dn_ref[pl.ds(pl.multiple_of(c * STATE, STATE), STATE), lanes] = ds
-            s_ref[:, lanes] = ds * own_pair(decay, 2 * q) + dot(cc, dyg, ((0,), (0,)))
+            s_ref[:, lanes] = ds * own_pair(decay, 2 * q)
+        s_ref[...] += dot(cc, dyg_ref[rows, :], ((0,), (0,)))
         return 0
 
     lax.fori_loop(0, spans, local_states, 0)
@@ -1257,7 +1282,7 @@
         mask = (col >= row) & (segc_ref[pl.ds(pl.multiple_of(FRONT + c * SPAN, FRONT), SPAN), :] == segr_ref[pl.ds(c, 1), :])
         lane = lax.broadcasted_iota(jnp.int32, (SPAN, LANES), 1)
         d_scores = jnp.zeros((SPAN, SPAN), f32)
-        dc = jnp.zeros((SPAN, STATE), f32)
+        dc = dot(dyg_ref[rows, :], st_ref[c].astype(bf16), ((1,), (1,)))
         for q in range(PAIRS):
             lanes = slice(q * LANES, (q + 1) * LANES)
             x = x_ref[rows, lanes]
@@ -1273,7 +1298,6 @@
                 d_weights = dot(jnp.where(own, xf, 0.0).astype(bf16), dy, ((1,), (1,)))
                 d_scores = d_scores + d_weights * decay_mat
             dxi_ref[rows, lanes] = jnp.where(lane < HEADDIM, parts[0], parts[1])
-            dc = dc + dot(dyg_ref[rows, lanes], st_ref[c, :, lanes].astype(bf16), ((1,), (1,)))
             dskip_ref[0:1, lanes] += jnp.sum(dy.astype(f32) * xf, axis=0, keepdims=True)
         d_scores_b = d_scores.astype(bf16)
         dn_ref[side_at(c, 0)] = dot(d_scores_b, cc)
@@ -1295,7 +1319,7 @@
         decay = jnp.exp(last) * carry_ref[pl.ds(c, 1), :]
         b = b_ref[rows, :]
         db = dn_ref[side_at(c, 0)]
-        edges = []
+        edges, ds_all = [], []
         for q in range(PAIRS):
             lanes = slice(q * LANES, (q + 1) * LANES)
             xf = x_ref[rows, lanes].astype(f32)
@@ -1306,7 +1330,8 @@
             ds = dn_ref[pl.ds(pl.multiple_of(c * STATE, STATE), STATE), lanes] + entering
             s_ref[:, lanes] = entering * dec
             ds_b = ds.astype(bf16)
-            db = db + dot((xf * ew).astype(bf16), ds_b, ((1,), (1,)))
+            dyg_ref[rows, lanes] = (xf * ew).astype(bf16)
+            ds_all.append(ds_b)
             dx_state = dot(b, ds_b) * ew
             dx = dxi_ref[rows, lanes] + dx_state
             edges.append(
@@ -1317,6 +1342,7 @@
             prod_ref[SPAN : 2 * SPAN, lanes] = xf * dx
             d_x = (dx + dyf * chans_ref[0:1, lanes]).astype(bf16).astype(f32)
             dtot_ref[rows, lanes] = d_x * dtot_ref[rows, lanes]
+        db = db + dot(dyg_ref[rows, :], jnp.concatenate(ds_all, axis=1), ((1,), (1,)))
         dtot_ref[rows, HALF : HALF + STATE] = db * dtot_ref[rows, HALF : HALF + STATE]
         dtot_ref[rows, HALF + STATE :] = dn_ref[side_at(c, 1)] * dtot_ref[rows, HALF + STATE :]
         sums = own_sums(prod_ref[0 : 2 * SPAN, :])
@@ -1344,9 +1370,9 @@
 
     def convolve(c, _):
         rows = span_rows(c)
-        marks = marks_ref[rows, :]
         fore = pl.ds(pl.multiple_of(c * SPAN, SPAN), SPAN + FRONT)
         hind = pl.ds(pl.multiple_of(c * SPAN, SPAN), SPAN + TILE)
+        masks = [jnp.broadcast_to(marks_ref[hind, j : j + 1], (SPAN + TILE, LANES)) for j in range(RIM)]
         for k in range(CHANS // LANES):
             lanes = slice(k * LANES, (k + 1) * LANES)
             later = dtot_ref[hind, lanes]
@@ -1356,11 +1382,11 @@
             dtaps_ref[RIM : RIM + 1, lanes] += jnp.sum(own * earlier[FRONT:], axis=0, keepdims=True)
             dtaps_ref[CONV : CONV + 1, lanes] += jnp.sum(own, axis=0, keepdims=True)
             for j in range(RIM):
-                ahead = RIM - j
-                d_conv = d_conv + taps_ref[j : j + 1, lanes] * later[ahead : ahead + SPAN] * marks[:, 3 + j : 4 + j]
-                first = FRONT - ahead
+                lag = RIM - j
+                seen = later * masks[j]
+                d_conv = d_conv + taps_ref[j : j + 1, lanes] * seen[lag : lag + SPAN]
                 dtaps_ref[j : j + 1, lanes] += jnp.sum(
-                    own * earlier[first : first + SPAN] * marks[:, j : j + 1], axis=0, keepdims=True
+                    seen[0:SPAN] * earlier[FRONT - lag : FRONT - lag + SPAN], axis=0, keepdims=True
                 )
             dmain_ref[rows, lanes] = d_conv.astype(bf16)
         return 0
@@ -1448,7 +1474,7 @@
         dn_ref[kept, :] = mixer[:, k * HALF : (k + 1) * HALF]
         copies.keep(dn_ref.at[kept], mixer_out.at[:, pl.ds(k * HALF, HALF)])
     hid = h_ref[mixes.block(0), :].astype(f32)
-    valid = valid_ref[...]
+    valid = validc_ref[...]
     counts = [jnp.sum(valid * jnp.sum(v * v, axis=1, keepdims=True), axis=0, keepdims=True) for v in (hid, mixer)]
     counts.append(jnp.sum(valid, axis=0, keepdims=True))
     scalars = jnp.zeros((1, LANES), f32)
@@ -1533,16 +1559,20 @@
 
 
 def update_kernel(
-    hid_ref, mixer_ref, dx_ref, back_ref, pre_ref, gmain_ref, ggate_ref, gout_ref, total_ref,
+    hid_ref, mixer_ref, dx_ref, back_ref, gmain_ref, ggate_ref, gout_ref, total_ref,
     inw_ref, inm_ref, inv_ref, outw_ref, outm_ref, outv_ref, small_ref, smallm_ref, smallv_ref,
     output_ref, gh_ref, inm_out, inv_out, inw_out, outm_out, outv_out, outw_out, smallm_out, smallv_out, smallw_out, rms_ref,
 ):
     hid = hid_ref[...].astype(f32)
     output_ref[...] = (hid + mixer_ref[...]).astype(bf16)
     scale = lax.rsqrt(jnp.sum(hid * hid, axis=1, keepdims=True) / D + norm_eps)
-    d_pre = dx_ref[...] * pre_ref[...]
-    pulled = jnp.sum(hid * d_pre, axis=1, keepdims=True) / D * (scale * scale * scale)
-    gh_ref[...] = back_ref[...].astype(f32) + scale * d_pre - hid * pulled
+    pulled = 0.0
+    for k in range(NORM_ROW):
+        lanes = slice(k * LANES, (k + 1) * LANES)
+        d_pre = dx_ref[:, lanes] * small_ref[k : k + 1, :]
+        gh_ref[:, lanes] = back_ref[:, lanes].astype(f32) + scale * d_pre
+        pulled = pulled + jnp.sum(hid[:, lanes] * d_pre, axis=1, keepdims=True)
+    gh_ref[...] -= hid * (pulled / D * (scale * scale * scale))
 
     def update(refs, outs, cols, grad, rate=0.02, decay=0.1):
         weight, moment, second = (ref[:, cols] for ref in refs)
@@ -1576,6 +1606,7 @@
     return pl.pallas_call(
         kernel,
         name=name,
+        grid=(1,),
         in_specs=in_specs,
         out_shape=tuple(o for o, _ in outs),
         out_specs=tuple(s for _, s in outs),
@@ -1589,22 +1620,16 @@
 def shards_linked(
     hidden, cotangent, segments, valid, in_w, in_m, in_v, out_w, out_m, out_v, small_w, small_m, small_v,
 ):
-    part = lax.axis_index("part")
     own_rows, out_rows = in_w.shape[0], out_w.shape[0]
     tok_rows = hidden.shape[1]
     rows = tok_rows * TP
     spans = rows // SPAN
-    edge = jnp.full((FRONT,), -1, jnp.int32)
-    seg_wide = lax.dynamic_slice_in_dim(jnp.concatenate([edge, segments[0], edge]), part * rows, rows + 2 * FRONT)
-    seg_spans = seg_wide[FRONT : FRONT + rows].reshape(spans, SPAN)
-    valid_col = valid[0].astype(f32)[:, None]
     small_size = small_w.shape[0]
 
     def small_box(array):
         return jnp.pad(array, (0, SMALL_ROWS * LANES - small_size)).reshape(SMALL_ROWS, LANES)
 
     small_w, small_m, small_v = small_box(small_w), small_box(small_m), small_box(small_v)
-    pre_row = small_w[:NORM_ROW].reshape(1, D)
 
     wide = (rows, D)
     half = (rows, HALF)
@@ -1646,7 +1671,7 @@
         ((TILE, CHANS), f32),
         ((TILE, LANES), f32),
         ((TILE, HALF), f32),
-        ((rows, TILE), f32),
+        ((rows + TILE, TILE), f32),
         ((spans, LANES), f32),
         (state, f32),
         (state, bf16),
@@ -1669,9 +1694,13 @@
         ((4, OWN_ROWS, LANES), f32),
         ((3, 3, OWN_ROWS, LANES), f32),
         ((D // 2, MAIN), bf16),
+        ((rows + 2 * FRONT, 1), f32),
+        ((TILE, SPAN), f32),
+        ((tok_rows, 1), f32),
     )
+    side_cols = pl.BlockSpec((own_rows, MAIN - HALF), lambda i: (0, 2 * D_INNER // (MAIN - HALF)))
     back_own, mixer, g_gate, g_main, d_x_normed, g_out, totals = linked(
-        functools.partial(main_kernel, spans), "main", 1, [*[HBM] * 4, *[VMEM] * 5], main_outs,
+        functools.partial(main_kernel, spans), "main", 1, [*[HBM] * 4, side_cols, *[VMEM] * 3], main_outs,
         [
             *[pltpu.VMEM(dims, dtype) for dims, dtype in main_scratch],
             *sum_buffers(out_rows, D, False),
@@ -1681,9 +1710,9 @@
             *scatter_buffers(tok_rows),
             *sems(200, 48),
         ],
-    )(hidden[0], in_w, out_w, cotangent[0], in_w[:, 2 * D_INNER :], valid_col, small_w, seg_wide[:, None], seg_spans)
-
-    steps = own_rows // TILE
+    )(hidden[0], in_w, out_w, cotangent[0], in_w, valid, small_w, segments)
+
+    steps = own_rows // (2 * TILE)
 
     def cut(dims, axis=0):
         block = tuple(size // steps if k == axis else size for k, size in enumerate(dims))
@@ -1703,7 +1732,6 @@
         grid=(steps,),
         in_specs=[
             *[cut(tokens)] * 4,
-            fixed((1, D)),
             cut(g_main.shape, 2),
             cut(g_gate.shape, 2),
             cut(matrix_out),
@@ -1720,7 +1748,7 @@
         out_specs=[*[cut(dims) for dims in out_dims], *[fixed(small_dims)] * 3, fixed((TILE, LANES))],
         compiler_params=pltpu.CompilerParams(vmem_limit_bytes=VMEM_LIMIT),
     )(
-        hidden[0], mixer, d_x_normed, back_own, pre_row, g_main, g_gate, g_out, totals,
+        hidden[0], mixer, d_x_normed, back_own, g_main, g_gate, g_out, totals,
         in_w, in_m, in_v, out_w, out_m, out_v, small_w, small_m, small_v,
     )
     small_m_new, small_v_new, small_w_new = (

time: 205 us -> 194 us (0.946)
  local copies, waits for them, and re-layouts: 9.69 us -> 4.33 us
  Pallas kernels: 193 us -> 189 us
    pallas_call x1, Pallas kernels: 183 us -> 180 us  [shards_linked(): linked(functools.partial(main_kernel, spans), 'main', 1, [*[HBM] * 4, sid...]
    slice x3 -> x0, local copies, waits for them, and re-layouts: 2.29 us -> none  [the longest x1 1.52 us: shards_linked(): in_w[:, 2 * D_INNER:]]
where the time goes in v1:
time: 194 us
  Pallas kernels  189 us (97%)
  local copies, waits for them, and re-layouts  4.33 us (2%)
    pallas_call x1, Pallas kernels, shards_linked(): linked(functools.partial(main_kernel, spans), 'main', 1, [*[HBM] * 4, sid...  180 us
    pallas_call x1, Pallas kernels, shards_linked(): pl.pallas_call(update_kernel, name='update', grid=(steps,), in_specs=[*[c...  9.34 us

profile of v1, /device:TPU:0, one launch (start us, length us, event | category | flops | bytes accessed | tf_op | source)
XLA Modules:
  0.0 194.1 jit_solution(6851700807789398054)
XLA Ops:
  0.6 1.5 pad_bitcast_fusion.2.small_ref
  2.2 1.6 pad_bitcast_fusion
  3.8 179.8 %main.1 = (bf16[192,1536]{1,0:T(8,128)(2,1)}, f32[192,1536]{1,0:T(8,128)}, f32[2,2,48,768]{3,2,1,0:T(8,128)}, f32[2,2,48,1152]{3,2,1,0:T(8,128)}, f32[192,1536]{...) custom-call(bf16[192,1536]{1,0:T(8,128)(2,1)} %bitcast.18, f32[48,6448]{1,0:T(8,128)} %inw_ref.1, ...), custom_call_target="tpu_custom_call" | custom-call | tf_op jit(solution)/shard_map/main/pallas_call | solution.py:1702
  183.6 9.3 %update.1 = (bf16[192,1536]{1,0:T(8,128)(2,1)}, f32[192,1536]{1,0:T(8,128)}, f32[48,6448]{1,0:T(8,128)}, f32[48,6448]{1,0:T(8,128)}, f32[48,6448]{1,0:T(8,128)},...) custom-call(bf16[192,1536]{1,0:T(8,128)(2,1)} %bitcast.19, ...), custom_call_target="tpu_custom_call" | custom-call | tf_op jit(solution)/shard_map/update/pallas_call | solution.py:1729
  192.9 1.2 slice_bitcast_fusion

commit v2 on v1

--- a/solution.py
+++ b/solution.py
@@ -891,6 +891,32 @@
     ]
     loads.append(copies.keep(cot_hbm, cotv_ref))
 
+    side = inside_ref[:, 0 : SIDE + HEADS]
+    dt_cols = jnp.concatenate([side[:, SIDE:], jnp.zeros((own_rows, LANES - HEADS), f32)], axis=1)
+    for copy in loads:
+        copies.settle(copy)
+
+    def master(first):
+        return gate_ref[first // HALF * own_rows : (first // HALF + 1) * own_rows, first % HALF : first % HALF + QUARTER]
+
+    for j in range(TP):
+        at = slice(j * own_rows, (j + 1) * own_rows)
+        for k, chans in enumerate(own_chans(j)):
+            part = slice(k * QUARTER, (k + 1) * QUARTER)
+            wg_ref[at, part] = master(chans.start).astype(bf16)
+            wm_ref[at, part] = master(D_INNER + chans.start).astype(bf16)
+        wm_ref[at, HALF:CHANS] = side[:, :SIDE].astype(bf16)
+        dt_own = (lane % (HEADS // 2) // (LOCAL_HEADS // 2) == j) & (lane < HEADS)
+        wm_ref[at, CHANS:MAIN] = jnp.where(dt_own, dt_cols, 0.0).astype(bf16)
+    for k in range(D // HALF):
+        wo_ref[:, k * HALF : (k + 1) * HALF] = dn_ref[k * out_rows : (k + 1) * out_rows, :].astype(bf16)
+
+    greeted(EVERY_NEIGHBOUR)
+    mains = WeightGather(copies, win_ref, own_rows, True)
+    mains.swap(wm_ref)
+    hids = GroupGather(copies, hid_ref, h_ref)
+    hids.start_t0()
+
     def column(row):
         return jnp.transpose(jnp.broadcast_to(row, (LANES, SPAN)))[:, 0:1]
 
@@ -906,33 +932,7 @@
     stat_ref[0] = jnp.zeros_like(stat_ref[0])
     stat_ref[0, 0:1, 0:tokens] = valid_ref[...].astype(f32)
     validc_ref[...] = column(stat_ref[0, 0:1, 0:SPAN])[0:tokens]
-
-    side = inside_ref[:, 0 : SIDE + HEADS]
-    dt_cols = jnp.concatenate([side[:, SIDE:], jnp.zeros((own_rows, LANES - HEADS), f32)], axis=1)
-    for copy in loads:
-        copies.settle(copy)
     cotv_ref[...] = (cotv_ref[...].astype(f32) * validc_ref[...]).astype(bf16)
-
-    def master(first):
-        return gate_ref[first // HALF * own_rows : (first // HALF + 1) * own_rows, first % HALF : first % HALF + QUARTER]
-
-    for j in range(TP):
-        at = slice(j * own_rows, (j + 1) * own_rows)
-        for k, chans in enumerate(own_chans(j)):
-            part = slice(k * QUARTER, (k + 1) * QUARTER)
-            wg_ref[at, part] = master(chans.start).astype(bf16)
-            wm_ref[at, part] = master(D_INNER + chans.start).astype(bf16)
-        wm_ref[at, HALF:CHANS] = side[:, :SIDE].astype(bf16)
-        dt_own = (lane % (HEADS // 2) // (LOCAL_HEADS // 2) == j) & (lane < HEADS)
-        wm_ref[at, CHANS:MAIN] = jnp.where(dt_own, dt_cols, 0.0).astype(bf16)
-    for k in range(D // HALF):
-        wo_ref[:, k * HALF : (k + 1) * HALF] = dn_ref[k * out_rows : (k + 1) * out_rows, :].astype(bf16)
-
-    greeted(EVERY_NEIGHBOUR)
-    mains = WeightGather(copies, win_ref, own_rows, True)
-    mains.swap(wm_ref)
-    hids = GroupGather(copies, hid_ref, h_ref)
-    hids.start_t0()
     copies.keep(cotv_ref, cotv_out)
 
     for k in range(HALF // LANES):
@@ -994,15 +994,15 @@
     norm(blocks[2])
     mains.hand_on()
     gates.spread_swapped()
+    outs = WeightGather(copies, wout_ref, out_rows, False)
+    outs.spread(wo_ref, ())
+    outs_kept = copies.keep(wo_ref, outs.mine(()))
     hids.finish()
     cots = GroupGather(copies, cotv_ref, back_ref)
     cots.start_t0()
     norm(blocks[1])
     norm(blocks[3])
     mains.hand_on_last()
-    outs = WeightGather(copies, wout_ref, out_rows, False)
-    outs.spread(wo_ref, ())
-    outs_kept = copies.keep(wo_ref, outs.mine(()))
     mains.finish()
     copies.settle(mains.kept)
 
@@ -1277,11 +1277,16 @@
         b = b_ref[rows, :]
         cc = c_ref[rows, :]
         scores = dot(b, cc, ((1,), (1,)))
-        row = lax.broadcasted_iota(jnp.int32, (SPAN, SPAN), 0)
-        col = lax.broadcasted_iota(jnp.int32, (SPAN, SPAN), 1)
-        mask = (col >= row) & (segc_ref[pl.ds(pl.multiple_of(FRONT + c * SPAN, FRONT), SPAN), :] == segr_ref[pl.ds(c, 1), :])
+        early, late = slice(0, SPAN // 2), slice(SPAN // 2, SPAN)
+        seg_col = segc_ref[pl.ds(pl.multiple_of(FRONT + c * SPAN, FRONT), SPAN), :]
+        seg_row = segr_ref[pl.ds(c, 1), :]
+        row = lax.broadcasted_iota(jnp.int32, (SPAN // 2, SPAN), 0)
+        col = lax.broadcasted_iota(jnp.int32, (SPAN // 2, SPAN), 1)
+        mask_early = (col >= row) & (seg_col[early] == seg_row)
+        mask_late = (col >= row)[:, early] & (seg_col[late] == seg_row[:, late])
         lane = lax.broadcasted_iota(jnp.int32, (SPAN, LANES), 1)
-        d_scores = jnp.zeros((SPAN, SPAN), f32)
+        d_early = jnp.zeros((SPAN // 2, SPAN), f32)
+        d_late = jnp.zeros((SPAN // 2, SPAN // 2), f32)
         dc = dot(dyg_ref[rows, :], st_ref[c].astype(bf16), ((1,), (1,)))
         for q in range(PAIRS):
             lanes = slice(q * LANES, (q + 1) * LANES)
@@ -1291,17 +1296,24 @@
             parts = []
             for k in range(2):
                 h = lane_of(2 * q + k)
-                gap = fore_log[h : h + 1, :] - back_log[:, h : h + 1]
-                decay_mat = jnp.exp(jnp.where(mask, gap, -1e30))
-                parts.append(dot((scores * decay_mat).astype(bf16), dy))
+                gap = fore_log[h : h + 1, :] - back_log[early, h : h + 1]
+                decay_early = jnp.exp(jnp.where(mask_early, gap, -1e30))
+                gap = fore_log[h : h + 1, late] - back_log[late, h : h + 1]
+                decay_late = jnp.exp(jnp.where(mask_late, gap, -1e30))
+                dx_early = dot((scores[early] * decay_early).astype(bf16), dy)
+                dx_late = dot((scores[late, late] * decay_late).astype(bf16), dy[late])
+                parts.append(jnp.concatenate([dx_early, dx_late], axis=0))
                 own = (lane < HEADDIM) if k == 0 else (lane >= HEADDIM)
-                d_weights = dot(jnp.where(own, xf, 0.0).astype(bf16), dy, ((1,), (1,)))
-                d_scores = d_scores + d_weights * decay_mat
+                x_own = jnp.where(own, xf, 0.0).astype(bf16)
+                d_early = d_early + dot(x_own[early], dy, ((1,), (1,))) * decay_early
+                d_late = d_late + dot(x_own[late], dy[late], ((1,), (1,))) * decay_late
             dxi_ref[rows, lanes] = jnp.where(lane < HEADDIM, parts[0], parts[1])
             dskip_ref[0:1, lanes] += jnp.sum(dy.astype(f32) * xf, axis=0, keepdims=True)
-        d_scores_b = d_scores.astype(bf16)
-        dn_ref[side_at(c, 0)] = dot(d_scores_b, cc)
-        dn_ref[side_at(c, 1)] = dc + dot(d_scores_b, b, ((0,), (0,)))
+        d_early_b, d_late_b = d_early.astype(bf16), d_late.astype(bf16)
+        dn_ref[side_at(c, 0)] = jnp.concatenate([dot(d_early_b, cc), dot(d_late_b, cc[late])], axis=0)
+        later = dot(d_early_b[:, late], b[early], ((0,), (0,))) + dot(d_late_b, b[late], ((0,), (0,)))
+        earlier = dot(d_early_b[:, early], b[early], ((0,), (0,)))
+        dn_ref[side_at(c, 1)] = dc + jnp.concatenate([earlier, later], axis=0)
         return 0
 
     lax.fori_loop(0, spans, inside, 0)
@@ -1560,8 +1572,8 @@
 
 def update_kernel(
     hid_ref, mixer_ref, dx_ref, back_ref, gmain_ref, ggate_ref, gout_ref, total_ref,
-    inw_ref, inm_ref, inv_ref, outw_ref, outm_ref, outv_ref, small_ref, smallm_ref, smallv_ref,
-    output_ref, gh_ref, inm_out, inv_out, inw_out, outm_out, outv_out, outw_out, smallm_out, smallv_out, smallw_out, rms_ref,
+    inw_ref, inm_ref, inv_ref, outw_ref, outm_ref, outv_ref, small_ref,
+    output_ref, gh_ref, inm_out, inv_out, inw_out, outm_out, outv_out, outw_out, rms_ref,
 ):
     hid = hid_ref[...].astype(f32)
     output_ref[...] = (hid + mixer_ref[...]).astype(bf16)
@@ -1595,9 +1607,6 @@
 
     @pl.when(pl.program_id(0) == 0)
     def _():
-        update(
-            (small_ref, smallm_ref, smallv_ref), (smallm_out, smallv_out, smallw_out), every, total_ref[0:SMALL_ROWS, :], 0.2, 0.0
-        )
         totals = total_ref[SMALL_ROWS:, :]
         rms_ref[...] = jnp.sqrt(totals / (totals[0:1, 2:3] * D))
 
@@ -1629,7 +1638,7 @@
     def small_box(array):
         return jnp.pad(array, (0, SMALL_ROWS * LANES - small_size)).reshape(SMALL_ROWS, LANES)
 
-    small_w, small_m, small_v = small_box(small_w), small_box(small_m), small_box(small_v)
+    small_rows = small_box(small_w)
 
     wide = (rows, D)
     half = (rows, HALF)
@@ -1710,7 +1719,7 @@
             *scatter_buffers(tok_rows),
             *sems(200, 48),
         ],
-    )(hidden[0], in_w, out_w, cotangent[0], in_w, valid, small_w, segments)
+    )(hidden[0], in_w, out_w, cotangent[0], in_w, valid, small_rows, segments)
 
     steps = own_rows // (2 * TILE)
 
@@ -1724,8 +1733,7 @@
     tokens, matrix_in, matrix_out, small_dims = (tok_rows, D), in_w.shape, out_w.shape, (SMALL_ROWS, LANES)
     out_dims = [tokens] * 2 + [matrix_in] * 3 + [matrix_out] * 3
     (
-        output, grad_hidden, in_m_new, in_v_new, in_w_new, out_m_new, out_v_new, out_w_new,
-        small_m_new, small_v_new, small_w_new, rms,
+        output, grad_hidden, in_m_new, in_v_new, in_w_new, out_m_new, out_v_new, out_w_new, rms,
     ) = pl.pallas_call(
         update_kernel,
         name="update",
@@ -1738,22 +1746,20 @@
             fixed((BOX_ROWS, LANES)),
             *[cut(matrix_in)] * 3,
             *[cut(matrix_out)] * 3,
-            *[fixed(small_dims)] * 3,
+            fixed(small_dims),
         ],
         out_shape=[
             *[shape(dims, bf16 if k == 0 else f32) for k, dims in enumerate(out_dims)],
-            *[shape(small_dims, f32)] * 3,
             shape((TILE, LANES), f32),
         ],
-        out_specs=[*[cut(dims) for dims in out_dims], *[fixed(small_dims)] * 3, fixed((TILE, LANES))],
+        out_specs=[*[cut(dims) for dims in out_dims], fixed((TILE, LANES))],
         compiler_params=pltpu.CompilerParams(vmem_limit_bytes=VMEM_LIMIT),
     )(
         hidden[0], mixer, d_x_normed, back_own, g_main, g_gate, g_out, totals,
-        in_w, in_m, in_v, out_w, out_m, out_v, small_w, small_m, small_v,
+        in_w, in_m, in_v, out_w, out_m, out_v, small_rows,
     )
-    small_m_new, small_v_new, small_w_new = (
-        array.reshape(-1)[:small_size] for array in (small_m_new, small_v_new, small_w_new)
-    )
+    small_grad = totals[:SMALL_ROWS].reshape(-1)[:small_size]
+    small_m_new, small_v_new, small_w_new = adamw(small_w, small_m, small_v, small_grad, 0.2, 0.0)
     return (
         output[None], grad_hidden[None], in_m_new, in_v_new, in_w_new, out_m_new, out_v_new, out_w_new,
         small_m_new, small_v_new, small_w_new, rms[0, :2],

time: 194 us -> 193 us (level)
  no operation moved by 1% of the time
where the time goes in v2:
time: 193 us; the launch traced here: 192 us
  Pallas kernels  188 us (97%)
  local copies, waits for them, and re-layouts  2.76 us (1%)
    pallas_call x1, Pallas kernels, shards_linked(): linked(functools.partial(main_kernel, spans), 'main', 1, [*[HBM] * 4, sid...  178 us
    pallas_call x1, Pallas kernels, shards_linked(): pl.pallas_call(update_kernel, name='update', grid=(steps,), in_specs=[*[c...  9.8 us

profile of v2, /device:TPU:0, one launch (start us, length us, event | category | flops | bytes accessed | tf_op | source)
XLA Modules:
  0.0 192.5 jit_solution(9246117656015015989)
XLA Ops:
  0.6 1.5 pad_bitcast_fusion.small_ref
  2.2 178.4 %main.1 = (bf16[192,1536]{1,0:T(8,128)(2,1)}, f32[192,1536]{1,0:T(8,128)}, f32[2,2,48,768]{3,2,1,0:T(8,128)}, f32[2,2,48,1152]{3,2,1,0:T(8,128)}, f32[192,1536]{...) custom-call(bf16[192,1536]{1,0:T(8,128)(2,1)} %bitcast.10, f32[48,6448]{1,0:T(8,128)} %inw_ref.1, ...), custom_call_target="tpu_custom_call" | custom-call | tf_op jit(solution)/shard_map/main/pallas_call | solution.py:1711
  180.6 0.0 copy-start
  180.6 0.0 copy-start.1
  180.6 0.0 copy-start.2
  180.7 0.0 copy-start.3
  180.7 9.8 %update.1 = (bf16[192,1536]{1,0:T(8,128)(2,1)}, f32[192,1536]{1,0:T(8,128)}, f32[48,6448]{1,0:T(8,128)}, f32[48,6448]{1,0:T(8,128)}, f32[48,6448]{1,0:T(8,128)},...) custom-call(bf16[192,1536]{1,0:T(8,128)(2,1)} %bitcast.11, ...), custom_call_target="tpu_custom_call" | custom-call | tf_op jit(solution)/shard_map/update/pallas_call | solution.py:1737
  190.5 1.2 slice_bitcast_fusion.1
  191.7 0.0 copy-done
  191.7 0.0 copy-done.1
  191.7 0.0 copy-done.2
  191.7 0.0 copy-done.3
  191.7 0.7 multiply_subtract_fusion
  (1 shorter events, 0.0 us)
Async XLA Ops:
  180.6 11.1 %copy-start = (f32[176,128]{1,0:T(8,128)S(1)}, f32[176,128]{1,0:T(8,128)}, u32[]{:S(2)}) copy-start(f32[176,128]{1,0:T(8,128)} %get-tuple-element.34.total_ref) | copy-start | bytes 270340
  180.6 11.1 %copy-start.1 = (f32[21392]{0:T(1024)S(1)}, f32[21392]{0:T(1024)}, u32[]{:S(2)}) copy-start(f32[21392]{0:T(1024)} %param.23) | copy-start | bytes 256708
  180.6 11.1 %copy-start.2 = (f32[21392]{0:T(1024)S(1)}, f32[21392]{0:T(1024)}, u32[]{:S(2)}) copy-start(f32[21392]{0:T(1024)} %param.25) | copy-start | bytes 256708
  180.7 11.1 %copy-start.3 = (f32[21392]{0:T(1024)S(1)}, f32[21392]{0:T(1024)}, u32[]{:S(2)}) copy-start(f32[21392]{0:T(1024)} %param.24) | copy-start | bytes 256708

commit v3 on v2

--- a/solution.py
+++ b/solution.py
@@ -1084,18 +1084,25 @@
         cum = cum_ref[rows, :]
         back_log = jnp.transpose(cum - jnp.log(dt_ref[rows, :]))
         scores = dot(c_ref[rows, :], b_ref[rows, :], ((1,), (1,)))
-        row = lax.broadcasted_iota(jnp.int32, (SPAN, SPAN), 0)
-        col = lax.broadcasted_iota(jnp.int32, (SPAN, SPAN), 1)
-        mask = (row >= col) & (segc_ref[pl.ds(pl.multiple_of(FRONT + c * SPAN, FRONT), SPAN), :] == segr_ref[pl.ds(c, 1), :])
+        early, late = slice(0, SPAN // 2), slice(SPAN // 2, SPAN)
+        seg_col = segc_ref[pl.ds(pl.multiple_of(FRONT + c * SPAN, FRONT), SPAN), :]
+        seg_row = segr_ref[pl.ds(c, 1), :]
+        row = lax.broadcasted_iota(jnp.int32, (SPAN // 2, SPAN), 0)
+        col = lax.broadcasted_iota(jnp.int32, (SPAN // 2, SPAN), 1)
+        mask_early = (row >= col)[:, early] & (seg_col[early] == seg_row[:, early])
+        mask_late = (row + SPAN // 2 >= col) & (seg_col[late] == seg_row)
         lane = lax.broadcasted_iota(jnp.int32, (SPAN, LANES), 1)
         for q in range(PAIRS):
             lanes = slice(q * LANES, (q + 1) * LANES)
             x = x_ref[rows, lanes]
             parts = []
             for h in (lane_of(2 * q), lane_of(2 * q + 1)):
-                gap = cum[:, h : h + 1] - back_log[h : h + 1, :]
-                weighted = scores * jnp.exp(jnp.where(mask, gap, -1e30))
-                parts.append(dot(weighted.astype(bf16), x))
+                gap = cum[early, h : h + 1] - back_log[h : h + 1, early]
+                weighted = scores[early, early] * jnp.exp(jnp.where(mask_early, gap, -1e30))
+                y_early = dot(weighted.astype(bf16), x[early])
+                gap = cum[late, h : h + 1] - back_log[h : h + 1, :]
+                weighted = scores[late] * jnp.exp(jnp.where(mask_late, gap, -1e30))
+                parts.append(jnp.concatenate([y_early, dot(weighted.astype(bf16), x)], axis=0))
             y_ref[rows, lanes] = jnp.where(lane < HEADDIM, parts[0], parts[1])
         return 0
 
@@ -1721,7 +1728,7 @@
         ],
     )(hidden[0], in_w, out_w, cotangent[0], in_w, valid, small_rows, segments)
 
-    steps = own_rows // (2 * TILE)
+    steps = own_rows // (3 * TILE)
 
     def cut(dims, axis=0):
         block = tuple(size // steps if k == axis else size for k, size in enumerate(dims))

time: 193 us -> 191 us (0.990)
  no operation moved by 1% of the time
where the time goes in v3:
time: 191 us
  Pallas kernels  187 us (98%)
  local copies, waits for them, and re-layouts  2.76 us (1%)
    pallas_call x1, Pallas kernels, shards_linked(): linked(functools.partial(main_kernel, spans), 'main', 1, [*[HBM] * 4, sid...  178 us
    pallas_call x1, Pallas kernels, shards_linked(): pl.pallas_call(update_kernel, name='update', grid=(steps,), in_specs=[*[c...  8.48 us

profile of v3, /device:TPU:0, one launch (start us, length us, event | category | flops | bytes accessed | tf_op | source)
XLA Modules:
  0.0 191.2 jit_solution(11857135257812924405)
XLA Ops:
  0.6 1.5 pad_bitcast_fusion.small_ref
  2.2 178.5 %main.1 = (bf16[192,1536]{1,0:T(8,128)(2,1)}, f32[192,1536]{1,0:T(8,128)}, f32[2,2,48,768]{3,2,1,0:T(8,128)}, f32[2,2,48,1152]{3,2,1,0:T(8,128)}, f32[192,1536]{...) custom-call(bf16[192,1536]{1,0:T(8,128)(2,1)} %bitcast.10, f32[48,6448]{1,0:T(8,128)} %inw_ref.1, ...), custom_call_target="tpu_custom_call" | custom-call | tf_op jit(solution)/shard_map/main/pallas_call | solution.py:1718
  180.7 0.0 copy-start
  180.7 0.0 copy-start.1
  180.7 0.0 copy-start.2
  180.7 0.0 copy-start.3
  180.7 8.5 %update.1 = (bf16[192,1536]{1,0:T(8,128)(2,1)}, f32[192,1536]{1,0:T(8,128)}, f32[48,6448]{1,0:T(8,128)}, f32[48,6448]{1,0:T(8,128)}, f32[48,6448]{1,0:T(8,128)},...) custom-call(bf16[192,1536]{1,0:T(8,128)(2,1)} %bitcast.11, ...), custom_call_target="tpu_custom_call" | custom-call | tf_op jit(solution)/shard_map/update/pallas_call | solution.py:1744
  189.2 1.2 slice_bitcast_fusion.1
  190.4 0.0 copy-done
  190.4 0.0 copy-done.1
  190.4 0.0 copy-done.2
  190.4 0.0 copy-done.3
  190.4 0.7 multiply_subtract_fusion
  (1 shorter events, 0.0 us)
Async XLA Ops:
  180.7 9.7 %copy-start = (f32[176,128]{1,0:T(8,128)S(1)}, f32[176,128]{1,0:T(8,128)}, u32[]{:S(2)}) copy-start(f32[176,128]{1,0:T(8,128)} %get-tuple-element.34.total_ref) | copy-start | bytes 270340
  180.7 9.7 %copy-start.1 = (f32[21392]{0:T(1024)S(1)}, f32[21392]{0:T(1024)}, u32[]{:S(2)}) copy-start(f32[21392]{0:T(1024)} %param.23) | copy-start | bytes 256708
  180.7 9.7 %copy-start.2 = (f32[21392]{0:T(1024)S(1)}, f32[21392]{0:T(1024)}, u32[]{:S(2)}) copy-start(f32[21392]{0:T(1024)} %param.25) | copy-start | bytes 256708
  180.7 9.7 %copy-start.3 = (f32[21392]{0:T(1024)S(1)}, f32[21392]{0:T(1024)}, u32[]{:S(2)}) copy-start(f32[21392]{0:T(1024)} %param.24) | copy-start | bytes 256708

commit v4 on v3

--- a/solution.py
+++ b/solution.py
@@ -76,12 +76,21 @@
     return pl.ds(pl.multiple_of(c * SPAN, SPAN), SPAN)
 
 
+def triangle_dot(mask, values):
+    high = values.astype(bf16)
+    rest = values - high.astype(f32)
+    middle = rest.astype(bf16)
+    low = (rest - middle.astype(f32)).astype(bf16)
+    sums = dot(mask.astype(bf16), jnp.concatenate([high, middle, low], axis=1))
+    width = values.shape[1]
+    return sums[:, :width] + (sums[:, width : 2 * width] + sums[:, 2 * width :])
+
+
 def span_decay(dt_ref, rate_ref, c, at=0):
     dt = dt_ref[span_rows(c), :]
     row = lax.broadcasted_iota(jnp.int32, (SPAN, SPAN), 0)
     col = lax.broadcasted_iota(jnp.int32, (SPAN, SPAN), 1)
-    lower = (row >= col).astype(f32)
-    return dt, dot(lower, dt * rate_ref[at : at + 1, :], precision=exact_prec)
+    return dt, triangle_dot(row >= col, dt * rate_ref[at : at + 1, :])
 
 
 def state_kernel(spans, x_ref, b_ref, dt_ref, rate_ref, keep_ref, carry_ref, s_ref, dec_ref):
@@ -253,8 +262,7 @@
         edge_sum = head_sums(jnp.broadcast_to(edge, (8, HALF)))[0:1]
         at_last = lax.broadcasted_iota(jnp.int32, (SPAN, LANES), 0) == SPAN - 1
         d_cum = out_sum - in_sum + jnp.where(at_last, edge_sum, 0.0)
-        upper = (col >= row).astype(f32)
-        d_log = dot(upper, d_cum, precision=exact_prec)
+        d_log = triangle_dot(col >= row, d_cum)
         drate_ref[0:1, :] += jnp.sum(d_log * dt, axis=0, keepdims=True)
         ddt_ref[rows, :] = d_log * rate_ref[0:1, :] * sig_ref[rows, :] + in_sum * ratio_ref[rows, :]
         return 0
@@ -1371,7 +1379,7 @@
         d_cum = out_sum - in_sum + jnp.where(at_last, edge_sum, 0.0)
         row = lax.broadcasted_iota(jnp.int32, (SPAN, SPAN), 0)
         col = lax.broadcasted_iota(jnp.int32, (SPAN, SPAN), 1)
-        d_log = dot((col >= row).astype(f32), d_cum, precision=exact_prec)
+        d_log = triangle_dot(col >= row, d_cum)
         z = z_ref[rows, :]
         small = jnp.exp(-jnp.abs(z))
         sig = jnp.where(z >= 0.0, 1.0, small) / (1.0 + small)

time: 191 us -> 191 us (level)
  no operation moved by 1% of the time
where the time goes in v4:
time: 191 us; the launch traced here: 190 us
  Pallas kernels  186 us (97%)
  local copies, waits for them, and re-layouts  2.76 us (1%)
    pallas_call x1, Pallas kernels, shards_linked(): linked(functools.partial(main_kernel, spans), 'main', 1, [*[HBM] * 4, sid...  178 us
    pallas_call x1, Pallas kernels, shards_linked(): pl.pallas_call(update_kernel, name='update', grid=(steps,), in_specs=[*[c...  8.48 us

profile of v4, /device:TPU:0, one launch (start us, length us, event | category | flops | bytes accessed | tf_op | source)
XLA Modules:
  0.0 190.4 jit_solution(303265508613117928)
XLA Ops:
  0.6 1.5 pad_bitcast_fusion.small_ref
  2.2 177.7 %main.1 = (bf16[192,1536]{1,0:T(8,128)(2,1)}, f32[192,1536]{1,0:T(8,128)}, f32[2,2,48,768]{3,2,1,0:T(8,128)}, f32[2,2,48,1152]{3,2,1,0:T(8,128)}, f32[192,1536]{...) custom-call(bf16[192,1536]{1,0:T(8,128)(2,1)} %bitcast.10, f32[48,6448]{1,0:T(8,128)} %inw_ref.1, ...), custom_call_target="tpu_custom_call" | custom-call | tf_op jit(solution)/shard_map/main/pallas_call | solution.py:1726
  179.9 0.0 copy-start
  179.9 0.0 copy-start.1
  179.9 0.0 copy-start.2
  179.9 0.0 copy-start.3
  180.0 8.5 %update.1 = (bf16[192,1536]{1,0:T(8,128)(2,1)}, f32[192,1536]{1,0:T(8,128)}, f32[48,6448]{1,0:T(8,128)}, f32[48,6448]{1,0:T(8,128)}, f32[48,6448]{1,0:T(8,128)},...) custom-call(bf16[192,1536]{1,0:T(8,128)(2,1)} %bitcast.11, ...), custom_call_target="tpu_custom_call" | custom-call | tf_op jit(solution)/shard_map/update/pallas_call | solution.py:1752
  188.4 1.2 slice_bitcast_fusion.1
  189.6 0.0 copy-done
  189.7 0.0 copy-done.1
  189.7 0.0 copy-done.2
  189.7 0.0 copy-done.3
  189.7 0.7 multiply_subtract_fusion
  (1 shorter events, 0.0 us)
Async XLA Ops:
  179.9 9.7 %copy-start = (f32[176,128]{1,0:T(8,128)S(1)}, f32[176,128]{1,0:T(8,128)}, u32[]{:S(2)}) copy-start(f32[176,128]{1,0:T(8,128)} %get-tuple-element.34.total_ref) | copy-start | bytes 270340
  179.9 9.7 %copy-start.1 = (f32[21392]{0:T(1024)S(1)}, f32[21392]{0:T(1024)}, u32[]{:S(2)}) copy-start(f32[21392]{0:T(1024)} %param.23) | copy-start | bytes 256708
  179.9 9.7 %copy-start.2 = (f32[21392]{0:T(1024)S(1)}, f32[21392]{0:T(1024)}, u32[]{:S(2)}) copy-start(f32[21392]{0:T(1024)} %param.25) | copy-start | bytes 256708
  179.9 9.7 %copy-start.3 = (f32[21392]{0:T(1024)S(1)}, f32[21392]{0:T(1024)}, u32[]{:S(2)}) copy-start(f32[21392]{0:T(1024)} %param.24) | copy-start | bytes 256708
